TPU v7x, 32 devices: a whole 2x2x4 slice. The times are simulated.
32 devices in a mesh: seq: 8 (over y, x, core), batch: 4 (over z).
Axes of the slice: x: 2, y: 2, z: 4, core: 2. Of those that a mesh axis runs over, the one named last changes fastest.
Arguments:
- tokens: bfloat16 [16, 4096, 768], P('batch', 'seq'), may hold values from -6 to 6
- w_in: bfloat16 [768, 3072], P(None, ('seq', 'batch')), may hold values from -0.21875 to 0.21875
- b_in: bfloat16 [3072], P(('seq', 'batch')), may hold values from -3 to 3
- w_out: bfloat16 [3072, 768], P(('seq', 'batch')), may hold values from -0.109375 to 0.109375
- b_out: bfloat16 [768], P(('seq', 'batch')), may hold values from -3 to 3
- gain_one: bfloat16 [768], P(('seq', 'batch')), may hold values from 0.099609375 to 1.8984375
- shift_one: bfloat16 [768], P(('seq', 'batch')), may hold values from -3 to 3
- gain_two: bfloat16 [768], P(('seq', 'batch')), may hold values from 0.099609375 to 1.8984375
- shift_two: bfloat16 [768], P(('seq', 'batch')), may hold values from -3 to 3
- cotangent: bfloat16 [16, 4096, 768], P('batch', 'seq'), may hold values from -6 to 6
Outputs:
- output: bfloat16 [16, 4096, 768], P('batch', 'seq')
- grad_tokens: bfloat16 [16, 4096, 768], P('batch', 'seq')
- grad_w_in: float32 [768, 3072], P(None, ('seq', 'batch'))
- grad_b_in: float32 [3072], P(('seq', 'batch'))
- grad_w_out: float32 [3072, 768], P(('seq', 'batch'))
- grad_b_out: float32 [768], P(('seq', 'batch'))
- grad_gain_one: float32 [768], P(('seq', 'batch'))
- grad_shift_one: float32 [768], P(('seq', 'batch'))
- grad_gain_two: float32 [768], P(('seq', 'batch'))
- grad_shift_two: float32 [768], P(('seq', 'batch'))
All inputs are finite; a program needn't handle non-finite values.
Results may differ from a plain program's by a relative error of at most 0.0076.
Values may be sent and summed in bfloat16 or wider, within the bound.
A program may use at most 384 MiB of HBM per device.

v0:
```python
from functools import partial
import math

import jax
import jax.numpy as jnp
from jax import lax
from jax.sharding import PartitionSpec as P

epsilon = 1e-05


def hidden_table(extent):
    idx_all = jnp.arange(extent, dtype=jnp.int32)
    angles = (idx_all[:, None] * idx_all[None, :] % extent).astype(jnp.float32) * (
        2.0 * math.pi / extent
    )
    factor = 1.0 / math.sqrt(extent)
    return jnp.concatenate([jnp.cos(angles) * factor, jnp.sin(angles) * factor], axis=1).astype(
        jnp.bfloat16
    )


def sequence_table(length):
    block_rows = min(512, length)
    block_count = length // block_rows
    col_ids = jnp.arange(length, dtype=jnp.int32)
    factor = 1.0 / math.sqrt(length)

    def table_rows(block_index):
        row_ids = block_index * block_rows + jnp.arange(block_rows, dtype=jnp.int32)
        angles = (row_ids[:, None] * col_ids[None, :] % length).astype(jnp.float32) * (
            2.0 * math.pi / length
        )
        return (jnp.stack([jnp.cos(angles), -jnp.sin(angles)]) * factor).astype(jnp.bfloat16)

    blocks = lax.map(table_rows, jnp.arange(block_count, dtype=jnp.int32))
    return jnp.moveaxis(blocks, 1, 0).reshape(2, length, length)


def normalize(values, gain, shift):
    center = values - jnp.mean(values, axis=-1, keepdims=True)
    inv_std = lax.rsqrt(jnp.mean(center * center, axis=-1, keepdims=True) + epsilon)
    normed = center * inv_std
    return (normed * gain + shift, normed, inv_std)


def norm_back(grad_out, normed, inv_std, gain):
    scaled = grad_out * gain
    centered = scaled - jnp.mean(scaled, axis=-1, keepdims=True)
    return inv_std * (centered - normed * jnp.mean(scaled * normed, axis=-1, keepdims=True))


def local(tokens, w_in, b_in, w_out, b_out, gain_one, shift_one, gain_two, shift_two, cotangent):
    batch_rows, seq_part, model_width = tokens.shape
    length = seq_part * lax.axis_size("seq")
    w_in_all, b_in_all, w_out_all, b_out_all, g_one_all, s_one_all, g_two_all, s_two_all = (
        lax.all_gather(w_in, ("seq", "batch"), axis=1, tiled=True),
        lax.all_gather(b_in, ("seq", "batch"), axis=0, tiled=True),
        lax.all_gather(w_out, ("seq", "batch"), axis=0, tiled=True),
        lax.all_gather(b_out, ("seq", "batch"), axis=0, tiled=True),
        lax.all_gather(gain_one, ("seq", "batch"), axis=0, tiled=True),
        lax.all_gather(shift_one, ("seq", "batch"), axis=0, tiled=True),
        lax.all_gather(gain_two, ("seq", "batch"), axis=0, tiled=True),
        lax.all_gather(shift_two, ("seq", "batch"), axis=0, tiled=True),
    )
    h_table = hidden_table(model_width)
    s_table = sequence_table(length)
    flat_tokens = tokens.reshape(-1, model_width)
    spectra = jnp.dot(flat_tokens, h_table, preferred_element_type=jnp.float32).astype(jnp.bfloat16)
    spectra = spectra.reshape(batch_rows, seq_part, 2, model_width)
    mixed_cols = jnp.einsum(
        "plm,bmpc->blc",
        s_table,
        lax.all_to_all(spectra, "seq", split_axis=3, concat_axis=1, tiled=True),
        preferred_element_type=jnp.float32,
    ).astype(jnp.bfloat16)
    mixed = lax.all_to_all(mixed_cols, "seq", split_axis=1, concat_axis=2, tiled=True)
    resid_one = flat_tokens.astype(jnp.float32) + mixed.reshape(-1, model_width).astype(jnp.float32)
    act_one, normed_one, inv_one = normalize(
        resid_one, g_one_all.astype(jnp.float32), s_one_all.astype(jnp.float32)
    )
    act_low = act_one.astype(jnp.bfloat16)
    pre_act = jnp.dot(act_low, w_in_all, preferred_element_type=jnp.float32) + b_in_all.astype(
        jnp.float32
    )
    activ, gelu_back = jax.vjp(partial(jax.nn.gelu, approximate=True), pre_act)
    hidden_low = activ.astype(jnp.bfloat16)
    branch = jnp.dot(hidden_low, w_out_all, preferred_element_type=jnp.float32) + b_out_all.astype(
        jnp.float32
    )
    resid_two = act_one + branch
    result, normed_two, inv_two = normalize(
        resid_two, g_two_all.astype(jnp.float32), s_two_all.astype(jnp.float32)
    )
    grad_out = cotangent.reshape(-1, model_width).astype(jnp.float32)
    grad_g_two = jnp.sum(grad_out * normed_two, axis=0)
    grad_s_two = jnp.sum(grad_out, axis=0)
    grad_r_two = norm_back(grad_out, normed_two, inv_two, g_two_all.astype(jnp.float32))
    grad_branch = grad_r_two.astype(jnp.bfloat16)
    grad_b_out = jnp.sum(grad_branch.astype(jnp.float32), axis=0)
    grad_w_out = jnp.einsum(
        "tf,td->fd", hidden_low, grad_branch, preferred_element_type=jnp.float32
    )
    grad_hidden = jnp.einsum(
        "td,fd->tf", grad_branch, w_out_all, preferred_element_type=jnp.float32
    )
    grad_pre = gelu_back(grad_hidden)[0].astype(jnp.bfloat16)
    grad_b_in = jnp.sum(grad_pre.astype(jnp.float32), axis=0)
    grad_w_in = jnp.einsum("td,tf->df", act_low, grad_pre, preferred_element_type=jnp.float32)
    grad_a_one = grad_r_two + jnp.einsum(
        "tf,df->td", grad_pre, w_in_all, preferred_element_type=jnp.float32
    )
    grad_g_one = jnp.sum(grad_a_one * normed_one, axis=0)
    grad_s_one = jnp.sum(grad_a_one, axis=0)
    grad_r_one = norm_back(grad_a_one, normed_one, inv_one, g_one_all.astype(jnp.float32))
    grad_mix = grad_r_one.astype(jnp.bfloat16).reshape(batch_rows, seq_part, model_width)
    spec_grad = jnp.einsum(
        "plm,blc->bmpc",
        s_table,
        lax.all_to_all(grad_mix, "seq", split_axis=2, concat_axis=1, tiled=True),
        preferred_element_type=jnp.float32,
    ).astype(jnp.bfloat16)
    grad_spec = lax.all_to_all(spec_grad, "seq", split_axis=1, concat_axis=3, tiled=True)
    grad_flat = grad_r_one + jnp.einsum(
        "te,de->td",
        grad_spec.reshape(-1, 2 * model_width),
        h_table,
        preferred_element_type=jnp.float32,
    )
    sum_w_in, sum_b_in, sum_w_out, sum_b_out, sum_g_one, sum_s_one, sum_g_two, sum_s_two = (
        lax.psum_scatter(grad_w_in, ("seq", "batch"), scatter_dimension=1, tiled=True),
        lax.psum_scatter(grad_b_in, ("seq", "batch"), scatter_dimension=0, tiled=True),
        lax.psum_scatter(grad_w_out, ("seq", "batch"), scatter_dimension=0, tiled=True),
        lax.psum_scatter(grad_b_out, ("seq", "batch"), scatter_dimension=0, tiled=True),
        lax.psum_scatter(grad_g_one, ("seq", "batch"), scatter_dimension=0, tiled=True),
        lax.psum_scatter(grad_s_one, ("seq", "batch"), scatter_dimension=0, tiled=True),
        lax.psum_scatter(grad_g_two, ("seq", "batch"), scatter_dimension=0, tiled=True),
        lax.psum_scatter(grad_s_two, ("seq", "batch"), scatter_dimension=0, tiled=True),
    )
    output = result.astype(jnp.bfloat16).reshape(batch_rows, seq_part, model_width)
    grad_tokens = grad_flat.astype(jnp.bfloat16).reshape(batch_rows, seq_part, model_width)
    return (
        output,
        grad_tokens,
        sum_w_in,
        sum_b_in,
        sum_w_out,
        sum_b_out,
        sum_g_one,
        sum_s_one,
        sum_g_two,
        sum_s_two,
    )


def solution(mesh):
    return jax.shard_map(
        local,
        mesh=mesh,
        in_specs=(
            P("batch", "seq", None),
            P(None, ("seq", "batch")),
            P(("seq", "batch")),
            P(("seq", "batch"), None),
            P(("seq", "batch")),
            P(("seq", "batch")),
            P(("seq", "batch")),
            P(("seq", "batch")),
            P(("seq", "batch")),
            P("batch", "seq", None),
        ),
        out_specs=(
            P("batch", "seq", None),
            P("batch", "seq", None),
            P(None, ("seq", "batch")),
            P(("seq", "batch")),
            P(("seq", "batch"), None),
            P(("seq", "batch")),
            P(("seq", "batch")),
            P(("seq", "batch")),
            P(("seq", "batch")),
            P(("seq", "batch")),
        ),
        check_vma=False,
    )
```

profile of v0, /device:TPU:0, one launch (start us, length us, event | category | flops | bytes accessed | tf_op | source)
XLA Modules:
  0.0 1000.7 jit_solution(16399185255194381789)
XLA Ops:
  7.9 10.0 %multiply_convert_fusion.1 = (bf16[768,768]{1,0:T(8,128)(2,1)S(1)}, bf16[768,768]{1,0:T(8,128)(2,1)S(1)}) fusion(), kind=kLoop, calls=%fused_computation.70 | loop fusion | flops 7667712 | bytes 2359296 | tf_op jit(solution)/shard_map/convert.8
  19.3 8.9 fusion.22
  28.3 11.2 %reshape.336 = bf16[4,512,2,768]{1,0,3,2:T(4,128)(2,1)} reshape(bf16[2048,1536]{0,1:T(8,128)(2,1)} %fusion.22) | data formatting | bytes 12582912 | tf_op jit(solution)/shard_map/reshape | solution.py:70
  39.4 7.6 copy.57
  53.1 307.0 %while.13 = (s32[]{:T(128)}, bf16[8,2,512,4096]{3,2,0,1:T(8,128)(2,1)}, s32[8]{0:T(128)S(1)}, s32[]{:T(128)}, s32[1]{0:T(128)}) while((s32[]{:T(128)}, bf16[8,2,512,4096]{3,2,0,1:T(8,128)(2,1)}, s32[8]{0:T(128)S(1)}, s32[]{:T(128)}, s32[1]{0:T(128)}) %tuple.48), condition=%wide.region_1.2_spmd.clone, body=%wide.region_0.1_spmd.clone.sunk | while | flops 44040704 | bytes 41947736 | solution.py:36
  54.3 33.0 %cosine_bitcast_fusion.2 = (f32[1,1,512,4096]{3,2,1,0:T(8,128)S(1)}, f32[1,1,512,4096]{3,2,1,0:T(8,128)S(1)}) fusion(s32[512]{0:T(512)S(1)} %iota_add_fusion.2), kind=kLoop, calls=%fused_computation.15.clone.1 | loop fusion | flops 31457280 | bytes 16779264 | tf_op jit(solution)/shard_map/while/body/eval_jaxpr/stack | solution.py:34
  92.7 33.0 %cosine_bitcast_fusion.2 = (f32[1,1,512,4096]{3,2,1,0:T(8,128)S(1)}, f32[1,1,512,4096]{3,2,1,0:T(8,128)S(1)}) fusion(s32[512]{0:T(512)S(1)} %iota_add_fusion.2), kind=kLoop, calls=%fused_computation.15.clone.1 | loop fusion | flops 31457280 | bytes 16779264 | tf_op jit(solution)/shard_map/while/body/eval_jaxpr/stack | solution.py:34
  131.0 33.0 %cosine_bitcast_fusion.2 = (f32[1,1,512,4096]{3,2,1,0:T(8,128)S(1)}, f32[1,1,512,4096]{3,2,1,0:T(8,128)S(1)}) fusion(s32[512]{0:T(512)S(1)} %iota_add_fusion.2), kind=kLoop, calls=%fused_computation.15.clone.1 | loop fusion | flops 31457280 | bytes 16779264 | tf_op jit(solution)/shard_map/while/body/eval_jaxpr/stack | solution.py:34
  169.3 33.0 %cosine_bitcast_fusion.2 = (f32[1,1,512,4096]{3,2,1,0:T(8,128)S(1)}, f32[1,1,512,4096]{3,2,1,0:T(8,128)S(1)}) fusion(s32[512]{0:T(512)S(1)} %iota_add_fusion.2), kind=kLoop, calls=%fused_computation.15.clone.1 | loop fusion | flops 31457280 | bytes 16779264 | tf_op jit(solution)/shard_map/while/body/eval_jaxpr/stack | solution.py:34
  207.6 33.0 %cosine_bitcast_fusion.2 = (f32[1,1,512,4096]{3,2,1,0:T(8,128)S(1)}, f32[1,1,512,4096]{3,2,1,0:T(8,128)S(1)}) fusion(s32[512]{0:T(512)S(1)} %iota_add_fusion.2), kind=kLoop, calls=%fused_computation.15.clone.1 | loop fusion | flops 31457280 | bytes 16779264 | tf_op jit(solution)/shard_map/while/body/eval_jaxpr/stack | solution.py:34
  246.0 33.0 %cosine_bitcast_fusion.2 = (f32[1,1,512,4096]{3,2,1,0:T(8,128)S(1)}, f32[1,1,512,4096]{3,2,1,0:T(8,128)S(1)}) fusion(s32[512]{0:T(512)S(1)} %iota_add_fusion.2), kind=kLoop, calls=%fused_computation.15.clone.1 | loop fusion | flops 31457280 | bytes 16779264 | tf_op jit(solution)/shard_map/while/body/eval_jaxpr/stack | solution.py:34
  284.3 33.0 %cosine_bitcast_fusion.2 = (f32[1,1,512,4096]{3,2,1,0:T(8,128)S(1)}, f32[1,1,512,4096]{3,2,1,0:T(8,128)S(1)}) fusion(s32[512]{0:T(512)S(1)} %iota_add_fusion.2), kind=kLoop, calls=%fused_computation.15.clone.1 | loop fusion | flops 31457280 | bytes 16779264 | tf_op jit(solution)/shard_map/while/body/eval_jaxpr/stack | solution.py:34
  322.6 33.0 %cosine_bitcast_fusion.2 = (f32[1,1,512,4096]{3,2,1,0:T(8,128)S(1)}, f32[1,1,512,4096]{3,2,1,0:T(8,128)S(1)}) fusion(s32[512]{0:T(512)S(1)} %iota_add_fusion.2), kind=kLoop, calls=%fused_computation.15.clone.1 | loop fusion | flops 31457280 | bytes 16779264 | tf_op jit(solution)/shard_map/while/body/eval_jaxpr/stack | solution.py:34
  360.0 8.9 copy.83
  369.0 10.4 %all_to_all.45 = bf16[4,4096,2,96]{1,3,2,0:T(8,128)(2,1)} reshape(bf16[4,8,512,2,96]{2,1,4,3,0:T(8,128)(2,1)} %bitcast.129) | data formatting | bytes 12582912 | tf_op jit(solution)/shard_map/all_to_all | solution.py:74
  379.4 35.6 %fusion.34 = bf16[4,4096,96]{1,2,0:T(8,128)(2,1)S(1)} fusion(bf16[4,4096,2,96]{1,3,2,0:T(8,128)(2,1)} %all_to_all.45, bf16[2,4096,4096,1]{2,1,0,3:T(8,128)(2,1)} %bitcast.6), kind=kOutput, calls=%fused_computation.63 | convolution fusion | flops 25771376640 | bytes 76546048 | tf_op jit(solution)/shard_map/plm,bmpc->blc/dot_general | solution.py:71
  431.0 77.4 %all-reduce.13 = (bf16[768]{0:T(1024)(128)(2,1)S(1)}, bf16[768]{0:T(1024)(128)(2,1)S(1)}, bf16[768]{0:T(1024)(128)(2,1)S(1)}, bf16[3072]{0:T(1024)(128)(2,1)S(1)...) all-reduce(bf16[768]{0:T(1024)(128)(2,1)S(1)} %dynamic-update-slice, ...), channel_id=1, replica_groups=mesh['seq'=8,'batch'=4] {'seq','batch'}, use_global_device_ids=true, to_apply=%add.3 | all-reduce | flops 6912 | bytes 27648
  525.7 6.3 copy.65
  531.9 9.7 copy.73
  547.5 9.7 reshape.364
  562.2 17.9 %fusion.43 = f32[2048,3072]{1,0:T(8,128)} fusion(bf16[768,3072]{0,1:T(8,128)(2,1)} %all-gather.3.cloned.1.call-done, f32[2048,768]{1,0:T(8,128)} %subtract_multiply_fusion.1, f32[768]{0:T(1024)S(1)} %convert_element_type.168, f32[768]{0:T(1024)S(1)} %convert_element_type.167), kind=kOutput, calls=%fused_computation.77 | convolution fusion | flops 9668395008 | bytes 36182016 | tf_op jit(solution)/shard_map/dot_general | solution.py:83
  580.1 23.1 %fusion.53 = (f32[2048]{0:T(1024)S(1)}, f32[2048,768]{1,0:T(8,128)S(1)}) fusion(f32[768]{0:T(1024)S(1)} %convert_element_type.172, bf16[3072,768]{1,0:T(8,128)(2,1)} %all-gather.5.cloned.1.call-done, f32[2048,3072]{1,0:T(8,128)} %fusion.43, f32[3072]{0:T(1024)S(1)} %convert_element_type.170, f32[768]{0:T(1024)S(1)} %convert_element_type.168, ...), kind=kOutput, calls=%fused_computation.93 | convolution fusion | flops 9734453248 | bytes 42497024 | tf_op jit(solution)/shard_map/dot_general | solution.py:88
  613.8 24.4 %fusion.47 = f32[3072,768]{1,0:T(8,128)} fusion(f32[2048,768]{1,0:T(8,128)} %get-tuple-element.100, f32[2048,3072]{1,0:T(8,128)} %fusion.43, f32[3072]{0:T(1024)S(1)} %convert_element_type.170), kind=kOutput, calls=%fused_computation.88 | convolution fusion | flops 9728163840 | bytes 40906752 | tf_op jit(solution)/shard_map/tf,td->fd/dot_general | solution.py:101
  638.2 34.5 %convert_reduce_fusion = (f32[3072]{0:T(1024)S(1)}, bf16[2048,3072]{1,0:T(8,128)(2,1)}) fusion(f32[2048,3072]{1,0:T(8,128)} %fusion.43, f32[3072]{0:T(1024)S(1)} %convert_element_type.170, bf16[3072,768]{1,0:T(8,128)(2,1)} %all-gather.5.cloned.1.call-done, f32[2048,768]{1,0:T(8,128)} %get-tuple-element.100), kind=kOutput, calls=%fused_computation.29 | convolution fusion | flops 9809949696 | bytes 48783360 | tf_op jit(solution)/shard_map/td,fd->tf/dot_general | solution.py:104
  672.7 17.5 %multiply_reduce_fusion = (f32[768]{0:T(1024)S(1)}, f32[2048]{0:T(1024)S(1)}, f32[2048]{0:T(1024)S(1)}, f32[768]{0:T(1024)S(1)}, f32[2048,768]{1,0:T(8,128)S(1)}) fusion(f32[2048,768]{1,0:T(8,128)S(1)} %bitcast.128, f32[768]{0:T(1024)S(1)} %convert_element_type.167, f32[2048,768]{1,0:T(8,128)} %get-tuple-element.100, ...), kind=kOutput, calls=%fused_computation.48 | convolution fusion | flops 9676253184 | bytes 36201472 | tf_op jit(solution)/shard_map/tf,df->td/dot_general | solution.py:110
  703.7 17.5 %fusion.41 = f32[768,3072]{0,1:T(8,128)} fusion(bf16[2048,3072]{1,0:T(8,128)(2,1)} %get-tuple-element.110, f32[2048,768]{1,0:T(8,128)} %subtract_multiply_fusion.1, f32[768]{0:T(1024)S(1)} %convert_element_type.168, f32[768]{0:T(1024)S(1)} %convert_element_type.167), kind=kOutput, calls=%fused_computation.76 | convolution fusion | flops 9668395008 | bytes 28317696 | tf_op jit(solution)/shard_map/td,tf->df/dot_general | solution.py:109
  721.3 28.6 %all-to-all-done.2 = bf16[4,512,768]{1,0,2:T(4,128)(2,1)S(1)} async-done(((bf16[4,512,768]{1,0,2:T(4,128)(2,1)}), bf16[4,512,768]{1,0,2:T(4,128)(2,1)S(1)}, u32[]{:S(2)}, u32[]{:S(2)}) %all-to-all-start.2) | async-done | bytes 3145760 | tf_op jit(solution)/shard_map/all_to_all | solution.py:120
  750.6 34.0 %fusion.30 = bf16[4,4096,2,96]{1,3,2,0:T(8,128)(2,1)} fusion(bf16[4,8,512,96,1]{2,3,1,4,0:T(8,128)(2,1)S(1)} %bitcast.136, bf16[8,2,512,4096]{3,2,0,1:T(8,128)(2,1)} %get-tuple-element.64), kind=kOutput, calls=%fused_computation.59 | convolution fusion | flops 25772949504 | bytes 76546048 | tf_op jit(solution)/shard_map/plm,blc->bmpc/dot_general | solution.py:117
  784.6 19.5 %copy.68 = bf16[4,4096,2,96]{3,2,0,1:T(2,128)(2,1)} copy(bf16[4,4096,2,96]{1,3,2,0:T(8,128)(2,1)} %fusion.30) | data formatting | bytes 12582912 | tf_op jit(solution)/shard_map/convert_element_type | solution.py:122
  809.1 142.7 %all-reduce.12 = (f32[3072]{0:T(1024)S(1)}, f32[768]{0:T(1024)S(1)}, f32[768]{0:T(1024)S(1)}, f32[768]{0:T(1024)S(1)}, f32[768]{0:T(1024)S(1)}, /*index=5*/f32[768]{0:T(1024)S(1)}) all-reduce(f32[3072]{0:T(1024)S(1)} %get-tuple-element.109, f32[768]{0:T(1024)S(1)} %copy-done.15, ...), channel_id=3, replica_groups=mesh['seq'=8,'batch'=4] {'seq','batch'}, use_global_device_ids=true, to_apply=%region_12.13.clone | all-reduce | flops 6912 | bytes 55296
  955.4 22.0 %copy.69 = bf16[4,8,512,2,96]{2,0,4,1,3:T(4,128)(2,1)} copy(bf16[4,8,512,2,96]{4,3,0,2,1:T(2,128)(2,1)} %bitcast.23) | data formatting | bytes 12582912 | tf_op jit(solution)/shard_map/all_to_all | solution.py:123
  983.0 10.6 %add_convert_fusion = bf16[2048,768]{1,0:T(8,128)(2,1)} fusion(bf16[2048,1536]{0,1:T(8,128)(2,1)S(1)} %bitcast.134, bf16[768,768]{1,0:T(8,128)(2,1)S(1)} %copy-done.8, bf16[768,768]{1,0:T(8,128)(2,1)S(1)} %copy-done.10, f32[2048,768]{1,0:T(8,128)} %subtract_multiply_fusion.1, f32[2048]{0:T(1024)S(1)} %broadcast_multiply_fusion, ...), kind=kOutput, calls=%fused_computation.50 | convolution fusion | flops 4847566848 | bytes 24407040 | tf_op jit(solution)/shard_map/te,de->td/dot_general | solution.py:124
  (145 shorter events, 127.8 us)
Async XLA Ops:
  7.2 555.0 %all-gather.3.cloned.1.call-start = ((), (), s32[]{:S(2)}) async-start(), calls=%async_computation.6 | async-start | bytes 4866048 | tf_op jit(solution)/shard_map/all_gather | solution.py:57
  17.9 1.0 copy-start.7
  18.0 1.4 copy-start.9
  47.0 313.1 %all-to-all-start = ((bf16[4,512,2,768]{1,0,2,3:T(4,128)(2,1)}), bf16[4,512,2,768]{1,0,2,3:T(4,128)(2,1)}, u32[]{:S(2)}, u32[]{:S(2)}) async-start(bf16[4,512,2,768]{1,0,2,3:T(4,128)(2,1)} %copy.57), calls=%async_computation | async-start | bytes 12582912 | tf_op jit(solution)/shard_map/all_to_all | solution.py:74
  52.3 527.8 %all-gather.5.cloned.1.call-start = ((), (), s32[]{:S(2)}) async-start(), calls=%async_computation.7 | async-start | bytes 4866048 | tf_op jit(solution)/shard_map/all_gather | solution.py:59
  419.7 9.8 copy-start.16
  419.7 10.0 %copy-start.17 = (bf16[24]{0:T(256)(128)(2,1)S(1)}, bf16[24]{0:T(256)(128)(2,1)}, u32[]{:S(2)}) copy-start(bf16[24]{0:T(256)(128)(2,1)} %param.18) | copy-start | bytes 148
  419.7 10.3 %copy-start.18 = (bf16[24]{0:T(256)(128)(2,1)S(1)}, bf16[24]{0:T(256)(128)(2,1)}, u32[]{:S(2)}) copy-start(bf16[24]{0:T(256)(128)(2,1)} %param.16) | copy-start | bytes 148
  419.7 10.5 %copy-start.19 = (bf16[24]{0:T(256)(128)(2,1)S(1)}, bf16[24]{0:T(256)(128)(2,1)}, u32[]{:S(2)}) copy-start(bf16[24]{0:T(256)(128)(2,1)} %param.19) | copy-start | bytes 148
  419.7 10.7 %copy-start.20 = (bf16[24]{0:T(256)(128)(2,1)S(1)}, bf16[24]{0:T(256)(128)(2,1)}, u32[]{:S(2)}) copy-start(bf16[24]{0:T(256)(128)(2,1)} %param.20) | copy-start | bytes 148
  419.8 10.9 %copy-start.21 = (bf16[96]{0:T(256)(128)(2,1)S(1)}, bf16[96]{0:T(256)(128)(2,1)}, u32[]{:S(2)}) copy-start(bf16[96]{0:T(256)(128)(2,1)} %param.14) | copy-start | bytes 580
  419.8 88.6 %copy-start.2 = (bf16[4,512,768]{2,1,0:T(8,128)(2,1)S(1)}, bf16[4,512,768]{2,1,0:T(8,128)(2,1)}, u32[]{:S(2)}) copy-start(bf16[4,512,768]{2,1,0:T(8,128)(2,1)} %param.21) | copy-start | bytes 9437188
  419.8 90.6 %all-to-all-start.1 = ((bf16[4,4096,96]{2,0,1:T(4,128)(2,1)}), bf16[4,4096,96]{2,0,1:T(4,128)(2,1)}, u32[]{:S(2)}, u32[]{:S(2)}) async-start(bf16[4,4096,96]{2,0,1:T(4,128)(2,1)} %copy.60), calls=%async_computation.1 | async-start | bytes 8388608 | tf_op jit(solution)/shard_map/all_to_all | solution.py:77
  424.8 568.8 %reduce-scatter.5.cloned.1.call-start = ((), (), s32[]{:S(2)}) async-start(), calls=%async_computation.9 | async-start | bytes 9732096 | tf_op jit(solution)/shard_map/reduce_scatter | solution.py:133
  522.9 2.7 copy-start
  531.9 9.7 copy-start.4
  541.6 4.6 copy-start.1
  547.4 9.8 copy-start.11
  547.4 9.7 copy-start.5
  603.2 1.9 copy-start.3
  638.1 34.6 %slice-start = ((s8[6291456]{0:T(1024)(128)(4,1)}), s8[2097152]{0:T(1024)(128)(4,1)S(1)}, s32[]{:S(2)}) async-start(s8[6291456]{0:T(1024)(128)(4,1)} %bitcast.127), calls=%async_computation.10 | async-start | bytes 4194304
  638.1 34.6 %slice-start.1 = ((s8[6291456]{0:T(1024)(128)(4,1)}), s8[4194304]{0:T(1024)(128)(4,1)S(1)}, s32[]{:S(2)}) async-start(s8[6291456]{0:T(1024)(128)(4,1)} %bitcast.127), calls=%async_computation.11 | async-start | bytes 8388608
  672.7 17.6 %copy-start.12 = (f32[1,4,4,128]{3,1,2,0:T(4,128)S(1)}, f32[1,4,4,128]{3,1,2,0:T(4,128)}, u32[]{:S(2)}) copy-start(f32[1,4,4,128]{3,1,2,0:T(4,128)} %copy-done.11) | copy-start | bytes 24580
  690.3 3.6 copy-start.6
  700.0 50.0 %all-to-all-start.2 = ((bf16[4,512,768]{1,0,2:T(4,128)(2,1)}), bf16[4,512,768]{1,0,2:T(4,128)(2,1)S(1)}, u32[]{:S(2)}, u32[]{:S(2)}) async-start(bf16[4,512,768]{1,0,2:T(4,128)(2,1)} %copy.66), calls=%async_computation.2 | async-start | bytes 6291456 | tf_op jit(solution)/shard_map/all_to_all | solution.py:120
  703.7 290.0 %reduce-scatter.3.cloned.1.call-start = ((), (), s32[]{:S(2)}) async-start(), calls=%async_computation.8 | async-start | bytes 9732096 | tf_op jit(solution)/shard_map/reduce_scatter | solution.py:131
  804.1 5.0 copy-start.13
  804.1 5.0 copy-start.14
  804.1 5.0 copy-start.15
  804.1 151.3 %all-to-all-start.3 = ((bf16[4,4096,2,96]{3,2,0,1:T(2,128)(2,1)}), bf16[4,4096,2,96]{3,2,0,1:T(2,128)(2,1)}, u32[]{:S(2)}, u32[]{:S(2)}) async-start(bf16[4,4096,2,96]{3,2,0,1:T(2,128)(2,1)} %copy.68), calls=%async_computation.3 | async-start | bytes 16777216 | tf_op jit(solution)/shard_map/all_to_all | solution.py:123
  977.4 5.6 copy-start.8
  977.4 5.6 copy-start.10
Sparse Core Ops, SparseCore 0:
  10.8 74.9 all-gather.2
  88.6 80.6 all-gather.4
  638.3 151.5 reduce-scatter.4
  797.2 171.7 reduce-scatter.2
where the time goes:
time: 1010 us; the launch traced here: 1000 us
  other arithmetic  332 us (33%)
  matrix products  224 us (22%)
  blocking collectives  220 us (22%)
  local copies, waits for them, and re-layouts  155 us (15%)
  waiting for transfers between devices  29.9 us (3%)
  starting transfers between devices  19.5 us (2%)
  between operations  14.7 us (1%)
    another operation x8, other arithmetic, table_rows(): jnp.stack([jnp.cos(angles), -jnp.sin(angles)]) * factor  264 us
    unnamed x2, blocking collectives  220 us
    dot_general x1, matrix products, local(): jnp.einsum('plm,bmpc->blc', s_table, lax.all_to_all(spectra, 'seq', split...  35.6 us
    dot_general x1, matrix products, local(): jnp.einsum('td,fd->tf', grad_branch, w_out_all, preferred_element_type=jn...  34.5 us
    dot_general x1, matrix products, local(): jnp.einsum('plm,blc->bmpc', s_table, lax.all_to_all(grad_mix, 'seq', spli...  34 us
    dynamic_update_slice x8, other arithmetic, sequence_table(): blocks = lax.map(table_rows, jnp.arange(block_count, dtype=jnp.int32))  32.2 us
    all_to_all x1, waiting for transfers between devices, local(): lax.all_to_all(grad_mix, 'seq', split_axis=2, concat_axis=1, tiled=True)  28.6 us
    unnamed x72, local copies, waits for them, and re-layouts  27.4 us
  transfers between devices with their start and end apart: 8, of which 1 were waited for; matrix products, arithmetic and copies ran while one was open for 64% of the time, Pallas kernels for 0%

commit v1 on v0

--- a/solution.py
+++ b/solution.py
@@ -3,10 +3,601 @@
 
 import jax
 import jax.numpy as jnp
+import ml_dtypes
+import numpy as np
 from jax import lax
+from jax.experimental import pallas as pl
+from jax.experimental.pallas import tpu as pltpu
 from jax.sharding import PartitionSpec as P
 
 epsilon = 1e-05
+f32, bf16 = jnp.float32, jnp.bfloat16
+MESH = pl.DeviceIdType.MESH
+
+
+def dot_nn(a, b):
+    return lax.dot_general(a, b, (((1,), (0,)), ((), ())), preferred_element_type=f32)
+
+
+def dot_nt(a, b):
+    return lax.dot_general(a, b, (((1,), (1,)), ((), ())), preferred_element_type=f32)
+
+
+def dot_tn(a, b):
+    return lax.dot_general(a, b, (((0,), (0,)), ((), ())), preferred_element_type=f32)
+
+
+def plan_columns(width, parts):
+    pairs = width // 2 // parts
+    r = np.arange(width)
+    dev, kind, i = r // (2 * pairs), (r // pairs) % 2, r % pairs
+    j = dev * pairs + i
+    first = (kind == 1) & (j == 0)
+    return j, kind, first
+
+
+def packed_hidden(width, parts):
+    j, kind, first = plan_columns(width, parts)
+    k = np.arange(width)
+    angle = (j[:, None] * k[None, :] % width) * (2.0 * math.pi / width)
+    table = np.where(kind[:, None] == 0, np.cos(angle), np.sin(angle))
+    nyquist = np.cos(np.pi * (k % 2))
+    table = np.where(first[:, None], nyquist[None, :], table) / math.sqrt(width)
+    return table.astype(np.float32).astype(ml_dtypes.bfloat16)
+
+
+def column_order(width, parts):
+    j, kind, first = plan_columns(width, parts)
+    col = np.where(kind == 0, j, np.where(first, width // 2, (width - j) % width))
+    return (col[:, None] == np.arange(width)[None, :]).astype(ml_dtypes.bfloat16)
+
+
+def inner_table(span, length):
+    a = np.arange(span)
+    angle = (a[:, None] * a[None, :] % span) * (2.0 * math.pi / span)
+    table = np.concatenate([np.cos(angle), np.sin(angle)], axis=0)
+    return (table / math.sqrt(length)).astype(np.float32).astype(ml_dtypes.bfloat16)
+
+
+def twiddles(parts, span):
+    b = np.arange(parts)[:, None]
+    angle = b * np.arange(span)[None, :] * (2.0 * math.pi / (parts * span))
+    return np.concatenate([np.cos(angle), np.sin(angle)], axis=0).astype(np.float32)
+
+
+def add(a, b):
+    return (a[0] + b[0], a[1] + b[1])
+
+
+def sub(a, b):
+    return (a[0] - b[0], a[1] - b[1])
+
+
+def minus_i(a):
+    return (a[1], -a[0])
+
+
+def dft4(x0, x1, x2, x3):
+    t0, t1, t2, t3 = add(x0, x2), sub(x0, x2), add(x1, x3), sub(x1, x3)
+    r = minus_i(t3)
+    return add(t0, t2), add(t1, r), sub(t0, t2), sub(t1, r)
+
+
+def dft8(x):
+    e = dft4(x[0], x[2], x[4], x[6])
+    o = dft4(x[1], x[3], x[5], x[7])
+    h = math.sqrt(0.5)
+    o1 = (h * (o[1][0] + o[1][1]), h * (o[1][1] - o[1][0]))
+    o2 = minus_i(o[2])
+    o3 = (h * (o[3][1] - o[3][0]), -h * (o[3][0] + o[3][1]))
+    o = (o[0], o1, o2, o3)
+    return [add(e[k], o[k]) for k in range(4)] + [sub(e[k], o[k]) for k in range(4)]
+
+
+def radix_step(rec, tw, t_ref, parts, pairs, span):
+    groups = pairs // 16
+    count = 2 * parts * pairs
+
+    def tile(u, carry):
+        lanes = pl.ds(pl.multiple_of(u * 128, 128), 128)
+        lanes_im = pl.ds(pl.multiple_of(span + u * 128, 128), 128)
+        extra = [jnp.zeros((16, 128), f32), jnp.zeros((16, 128), f32)]
+        row = lax.broadcasted_iota(jnp.int32, (16, 128), 0)
+        for g in range(groups):
+            x = []
+            for s in range(parts):
+                re = rec[s, g * 16:g * 16 + 16, lanes].astype(f32)
+                im = rec[s, pairs + g * 16:pairs + g * 16 + 16, lanes].astype(f32)
+                x.append((re, -im))
+            y = dft8(x)
+            for b in range(parts):
+                c, s = tw[b:b + 1, lanes], tw[parts + b:parts + b + 1, lanes]
+                conj = y[(parts - b) % parts]
+                for kind, (zr, zi) in enumerate((y[b], (conj[0], -conj[1]))):
+                    tr = c * zr + s * zi
+                    ti = c * zi - s * zr
+                    base = (kind * parts + b) * pairs + g * 16
+                    t_ref[base:base + 16, lanes] = tr.astype(bf16)
+                    t_ref[base:base + 16, lanes_im] = ti.astype(bf16)
+                    if g == 0:
+                        hit = row == kind * parts + b
+                        extra[0] = jnp.where(hit, jnp.broadcast_to(-ti[0:1], (16, 128)), extra[0])
+                        extra[1] = jnp.where(hit, jnp.broadcast_to(tr[0:1], (16, 128)), extra[1])
+        t_ref[count:count + 16, lanes] = extra[0].astype(bf16)
+        t_ref[count:count + 16, lanes_im] = extra[1].astype(bf16)
+        return carry
+
+    lax.fori_loop(0, span // 128, tile, 0)
+
+
+def spread_step(o_ref, put, me, parts, pairs, span, u):
+    count = 2 * parts * pairs
+    lanes = pl.ds(pl.multiple_of(u * 128, 128), 128)
+    low = lax.broadcasted_iota(jnp.int32, (16, 128), 1) < 64
+    row = lax.broadcasted_iota(jnp.int32, (16, 128), 0)
+    special = (row == 0) & (jnp.zeros((16, 128), jnp.int32) + me == 0)
+    extra = o_ref[count:count + 16, lanes]
+    for p in range(parts // 2):
+        for g in range(pairs // 16):
+            v = [[None, None], [None, None]]
+            for kind in range(2):
+                for h in range(2):
+                    base = (kind * parts + 2 * p + h) * pairs + g * 16
+                    v[kind][h] = o_ref[base:base + 16, lanes]
+            if g == 0:
+                for h in range(2):
+                    b = 2 * p + h
+                    even = 0.5 * (v[0][h] + v[1][h])
+                    odd = jnp.broadcast_to(0.5 * (extra[b:b + 1] - extra[parts + b:parts + b + 1]), (16, 128))
+                    v[0][h] = jnp.where(special, even, v[0][h])
+                    v[1][h] = jnp.where(special, odd, v[1][h])
+            for kind in range(2):
+                v0, v1 = v[kind]
+                rows = pl.ds(kind * pairs + g * 16, 16)
+                cols = pl.ds(p * 128, 128)
+                put(2 * u, rows, cols, jnp.where(low, v0, pltpu.roll(v1, 64, 1)).astype(bf16))
+                put(2 * u + 1, rows, cols, jnp.where(low, pltpu.roll(v0, 64, 1), v1).astype(bf16))
+
+
+def fold(v):
+    total = v[0:8]
+    for k in range(8, v.shape[0], 8):
+        total = total + v[k:k + 8]
+    return total
+
+
+def rows_of(ref, at):
+    return jnp.concatenate([ref[c, at, :] for c in range(ref.shape[0])], axis=1)
+
+
+def set_rows(ref, at, value):
+    for c in range(ref.shape[0]):
+        ref[c, at, :] = value[:, c * 128:(c + 1) * 128]
+
+
+def mean_of(v):
+    return jnp.mean(v, axis=-1, keepdims=True)
+
+
+def gelu_pair(x):
+    k = math.sqrt(2.0 / math.pi)
+    c = 0.044715
+    x2 = x * x
+    half = 0.5 + 0.5 * jnp.tanh(x * (k + (k * c) * x2))
+    value = x * half
+    slope = half + value * (1.0 - half) * (2.0 * k + (6.0 * k * c) * x2)
+    return value, slope
+
+
+def ffn_forward(x_get, nbuf, sbuf, alow, hid, slope, acc, w, vec, bias_in, chunk, rows_step):
+    rows = nbuf.shape[1]
+
+    def first(r, carry):
+        at = pl.ds(pl.multiple_of(r * rows_step, rows_step), rows_step)
+        v = x_get(at).astype(f32) + rows_of(nbuf, at)
+        center = v - mean_of(v)
+        inv = lax.rsqrt(mean_of(center * center) + epsilon)
+        n = center * inv
+        set_rows(nbuf, at, n)
+        sbuf[at, :] = jnp.broadcast_to(inv, (rows_step, 128))
+        alow[at, :] = (n * vec[0:1] + vec[1:2]).astype(bf16)
+        return carry
+
+    lax.fori_loop(0, rows // rows_step, first, 0)
+
+    def step(c, carry):
+        at = pl.ds(pl.multiple_of(c * chunk, chunk), chunk)
+        pre = dot_nt(alow[...], w[0, at, :]) + bias_in[c]
+        value, back = gelu_pair(pre)
+        low = value.astype(bf16)
+        hid[c] = low
+        slope[c] = back.astype(bf16)
+        part = dot_nn(low, w[1, at, :])
+
+        @pl.when(c == 0)
+        def _():
+            acc[...] = part
+
+        @pl.when(c > 0)
+        def _():
+            acc[...] += part
+
+        return carry
+
+    lax.fori_loop(0, hid.shape[0], step, 0)
+
+
+def ffn_middle(nbuf, acc, glow, cot, outv, vec, sums, rows_step):
+    rows = nbuf.shape[1]
+
+    def second(r, carry):
+        at = pl.ds(pl.multiple_of(r * rows_step, rows_step), rows_step)
+        v = rows_of(nbuf, at) * vec[0:1] + vec[1:2] + (acc[at, :] + vec[4:5])
+        center = v - mean_of(v)
+        inv = lax.rsqrt(mean_of(center * center) + epsilon)
+        n = center * inv
+        outv[at, :] = (n * vec[2:3] + vec[3:4]).astype(bf16)
+        g = cot[at, :].astype(f32)
+        q = g * vec[2:3]
+        gr = inv * (q - mean_of(q) - n * mean_of(q * n))
+        acc[at, :] = gr
+        low = gr.astype(bf16)
+        glow[at, :] = low
+        sums[2] += fold(g * n)
+        sums[3] += fold(g)
+        sums[4] += fold(low.astype(f32))
+        return carry
+
+    lax.fori_loop(0, rows // rows_step, second, 0)
+
+
+def ffn_backward(nbuf, sbuf, alow, hid, slope, acc, glow, w, dw, bsum, vec, sums, chunk, rows_step, put):
+    rows = nbuf.shape[1]
+
+    def step(c, carry):
+        at = pl.ds(pl.multiple_of(c * chunk, chunk), chunk)
+        gh = dot_nt(glow[...], w[1, at, :])
+        pre32 = gh * slope[c].astype(f32)
+        gpre = pre32.astype(bf16)
+        bsum[c] += fold(gpre.astype(f32))
+        dw[1, at, :] += dot_tn(hid[c], glow[...])
+        dw[0, at, :] += dot_tn(gpre, alow[...])
+        acc[...] += dot_nn(gpre, w[0, at, :])
+        return carry
+
+    lax.fori_loop(0, hid.shape[0], step, 0)
+
+    def last(r, carry):
+        at = pl.ds(pl.multiple_of(r * rows_step, rows_step), rows_step)
+        ga = acc[at, :]
+        n = rows_of(nbuf, at)
+        sums[0] += fold(ga * n)
+        sums[1] += fold(ga)
+        q = ga * vec[0:1]
+        put(at, sbuf[at, 0:1] * (q - mean_of(q) - n * mean_of(q * n)))
+        return carry
+
+    lax.fori_loop(0, rows // rows_step, last, 0)
+
+
+def layer_kernel(geo, tok, cot, w_all, hp_all, wd_all, cp_all, tw, vec, bias_in,
+                 out, gtok, grow, dw_all, small, bsum,
+                 tokv, cotv, outv, w, hp, wd, cp, dw, send1, recv1, send2, recv2, t_ref, o_ref,
+                 nbuf, sbuf, alow, hid, slope, acc, glow, sums,
+                 ss1, rs1, ss2, rs2, free1, free2, load, io):
+    parts, pairs, span, width, jobs, chunk, rows_step = geo
+    me = lax.axis_index("seq")
+    plane = lax.axis_index("batch")
+
+    def peer(d):
+        return lax.rem(me + d, parts)
+
+    def load_of(k):
+        if k < jobs:
+            return pltpu.make_async_copy(tok.at[k], tokv.at[k], load.at[k])
+        a, b = ((hp_all, hp), (wd_all, wd), (cp_all, cp), (w_all, w))[k - jobs]
+        return pltpu.make_async_copy(a, b, load.at[k])
+
+    for k in (jobs, 0, 1, jobs + 1, 2, 3, jobs + 2, jobs + 3):
+        load_of(k).start()
+
+    barrier = pltpu.get_barrier_semaphore()
+
+    def greet(d, carry):
+        pl.semaphore_signal(barrier, inc=1, device_id=(peer(d), plane), device_id_type=MESH)
+        return carry
+
+    lax.fori_loop(1, parts, greet, 0)
+    pl.semaphore_wait(barrier, parts - 1)
+
+    def remote(send, recv, ss, rs, k, d):
+        p = peer(d)
+        return pltpu.make_async_remote_copy(
+            src_ref=send.at[lax.rem(k, 2), p], dst_ref=recv.at[lax.rem(k, jobs), me],
+            send_sem=ss.at[lax.rem(k, 2), d], recv_sem=rs.at[lax.rem(k, jobs), d],
+            device_id=(p, plane), device_id_type=MESH)
+
+    def own(send, recv, rs, k):
+        return pltpu.make_async_copy(
+            send.at[lax.rem(k, 2), me], recv.at[lax.rem(k, jobs), me], rs.at[lax.rem(k, jobs), 0])
+
+    def wait_sends(send, recv, ss, rs, k):
+        def one(d, carry):
+            remote(send, recv, ss, rs, k, d).wait_send()
+            return carry
+
+        lax.fori_loop(1, parts, one, 0)
+
+    def wait_recvs(send, recv, ss, rs, k):
+        own(send, recv, rs, k).wait()
+
+        def one(d, carry):
+            source = lax.rem(me + parts - d, parts)
+            slot = lax.rem(k, jobs)
+            pltpu.make_async_remote_copy(
+                src_ref=send.at[0, 0], dst_ref=recv.at[slot, source],
+                send_sem=ss.at[0, d], recv_sem=rs.at[slot, d],
+                device_id=(source, plane), device_id_type=MESH).wait_recv()
+            return carry
+
+        lax.fori_loop(1, parts, one, 0)
+
+    def tell(sem, slot):
+        def one(d, carry):
+            pl.semaphore_signal(sem.at[slot], inc=1, device_id=(peer(d), plane), device_id_type=MESH)
+            return carry
+
+        lax.fori_loop(1, parts, one, 0)
+
+    one_way = (send1, recv1, ss1, rs1)
+    way_back = (send2, recv2, ss2, rs2)
+
+    def hidden_job(k):
+        table = dot_nt(hp[...], tokv[lax.rem(k, jobs)]).astype(bf16)
+        send1[lax.rem(k, 2)] = table.reshape(parts, 2 * pairs, span)
+        own(send1, recv1, rs1, k).start()
+
+        def one(d, carry):
+            remote(*one_way, k, d).start()
+            return carry
+
+        lax.fori_loop(1, parts, one, 0)
+
+    def sequence_job(k, before_send):
+        wait_recvs(*one_way, k)
+        radix_step(recv1.at[lax.rem(k, jobs)], tw, t_ref, parts, pairs, span)
+        o_ref[...] = dot_nn(t_ref[...], wd[...])
+        before_send()
+        slot = lax.rem(k, 2)
+
+        def one(u, carry):
+            def put(p, rows, cols, value):
+                send2[slot, p, rows, cols] = value
+
+            spread_step(o_ref, put, me, parts, pairs, span, u)
+            for h in range(2):
+                d = lax.rem(2 * u + h - me + parts, parts)
+
+                @pl.when(d > 0)
+                def _():
+                    remote(*way_back, k, d).start()
+
+                @pl.when(d == 0)
+                def _():
+                    own(send2, recv2, rs2, k).start()
+            return carry
+
+        lax.fori_loop(0, parts // 2, one, 0)
+
+    def mixed_job(k):
+        wait_recvs(*way_back, k)
+        blocks = recv2[lax.rem(k, jobs)].reshape(width, span)
+        natural = dot_tn(blocks, cp[...])
+        step = span // parts
+        for b in range(parts):
+            for c in range(width // 128):
+                nbuf[c, pl.ds(b, step, stride=parts), :] = natural[b * step:(b + 1) * step, c * 128:(c + 1) * 128]
+
+    load_of(jobs).wait()
+    for k in range(2):
+        load_of(k).wait()
+
+    def lead(k, carry):
+        hidden_job(k)
+        return carry
+
+    lax.fori_loop(0, 2, lead, 0)
+    dw[...] = jnp.zeros_like(dw)
+    sums[...] = jnp.zeros_like(sums)
+    bsum[...] = jnp.zeros_like(bsum)
+    for k in (2, 3, jobs + 1, jobs + 2):
+        load_of(k).wait()
+
+    def fill(k, carry):
+        sequence_job(k, lambda: None)
+        tell(free1, k)
+        wait_sends(*one_way, k)
+        hidden_job(k + 2)
+        return carry
+
+    lax.fori_loop(0, 2, fill, 0)
+    load_of(jobs + 3).wait()
+
+    def out_copy(i):
+        return pltpu.make_async_copy(outv, out.at[i], io.at[0])
+
+    def cot_copy(i):
+        return pltpu.make_async_copy(cot.at[i], cotv, io.at[1])
+
+    def row_copy(i):
+        return pltpu.make_async_copy(acc, grow.at[i], io.at[2])
+
+    def main(i, carry):
+        cot_copy(i).start()
+        mixed_job(i)
+        tell(free2, i)
+        ffn_forward(lambda at: tokv[i, at, :], nbuf, sbuf, alow, hid, slope, acc, w, vec, bias_in, chunk, rows_step)
+
+        def before():
+            wait_sends(*way_back, i)
+
+            @pl.when(i >= 2)
+            def _():
+                pl.semaphore_wait(free2.at[lax.rem(i + 2, jobs)], parts - 1)
+
+        sequence_job(i + 2, before)
+
+        @pl.when(i < 2)
+        def _():
+            tell(free1, lax.rem(i + 2, jobs))
+
+        cot_copy(i).wait()
+
+        @pl.when(i > 0)
+        def _():
+            out_copy(i - 1).wait()
+
+        ffn_middle(nbuf, acc, glow, cotv, outv, vec, sums, rows_step)
+        out_copy(i).start()
+
+        def put(at, value):
+            acc[at, :] = value
+            tokv[i, at, :] = value.astype(bf16)
+
+        ffn_backward(nbuf, sbuf, alow, hid, slope, acc, glow, w, dw, bsum, vec, sums, chunk, rows_step, put)
+        row_copy(i).start()
+        wait_sends(*one_way, i + 2)
+        pl.semaphore_wait(free1.at[i], parts - 1)
+        hidden_job(i + jobs)
+        row_copy(i).wait()
+        return carry
+
+    lax.fori_loop(0, jobs, main, 0)
+    dw_copy = pltpu.make_async_copy(dw, dw_all, io.at[3])
+    dw_copy.start()
+    small[...] = sums[...]
+
+    def gt_copy(i):
+        return pltpu.make_async_copy(tokv.at[i], gtok.at[i], io.at[4 + i])
+
+    def final(i):
+        back = pltpu.make_async_copy(grow.at[i], acc, io.at[2])
+        back.start()
+        mixed_job(i + jobs)
+        back.wait()
+        for c in range(width // 128):
+            tokv[i, :, c * 128:(c + 1) * 128] = (nbuf[c] + acc[:, c * 128:(c + 1) * 128]).astype(bf16)
+        gt_copy(i).start()
+
+    def drain(i, carry):
+        final(i)
+
+        def before():
+            wait_sends(*way_back, i + 4)
+            pl.semaphore_wait(free2.at[i + 2], parts - 1)
+
+        sequence_job(i + 6, before)
+        return carry
+
+    lax.fori_loop(0, 2, drain, 0)
+
+    def finish(i, carry):
+        final(i + 2)
+        wait_sends(*way_back, i + 6)
+        wait_sends(*one_way, i + 6)
+        return carry
+
+    lax.fori_loop(0, 2, finish, 0)
+    out_copy(jobs - 1).wait()
+    dw_copy.wait()
+    for i in range(jobs):
+        gt_copy(i).wait()
+
+
+def layer_call(tok, cot, w_all, vec, bias_in, parts):
+    jobs, span, width = tok.shape
+    ff = w_all.shape[1]
+    pairs = width // 2 // parts
+    chunk, rows_step = ff // 3, span // 2
+    steps = ff // chunk
+    length = span * parts
+    geo = (parts, pairs, span, width, jobs, chunk, rows_step)
+    tables = (
+        jnp.asarray(packed_hidden(width, parts)),
+        jnp.asarray(inner_table(span, length)),
+        jnp.asarray(column_order(width, parts)),
+        jnp.asarray(twiddles(parts, span)),
+    )
+    hbm, vmem, dma = pl.BlockSpec(memory_space=pl.ANY), pl.BlockSpec(memory_space=pltpu.VMEM), pltpu.SemaphoreType.DMA
+    block = (parts, 2 * pairs, span)
+    scratch = [
+        pltpu.VMEM((jobs, span, width), bf16),
+        pltpu.VMEM((span, width), bf16),
+        pltpu.VMEM((span, width), bf16),
+        pltpu.VMEM((2, ff, width), bf16),
+        pltpu.VMEM((width, width), bf16),
+        pltpu.VMEM((2 * span, span), bf16),
+        pltpu.VMEM((width, width), bf16),
+        pltpu.VMEM((2, ff, width), f32),
+        pltpu.VMEM((2,) + block, bf16),
+        pltpu.VMEM((jobs,) + block, bf16),
+        pltpu.VMEM((2,) + block, bf16),
+        pltpu.VMEM((jobs,) + block, bf16),
+        pltpu.VMEM((2 * parts * pairs + 16, 2 * span), bf16),
+        pltpu.VMEM((2 * parts * pairs + 16, span), f32),
+        pltpu.VMEM((width // 128, span, 128), f32),
+        pltpu.VMEM((span, 128), f32),
+        pltpu.VMEM((span, width), bf16),
+        pltpu.VMEM((steps, span, chunk), bf16),
+        pltpu.VMEM((steps, span, chunk), bf16),
+        pltpu.VMEM((span, width), f32),
+        pltpu.VMEM((span, width), bf16),
+        pltpu.VMEM((5, 8, width), f32),
+        dma((2, parts)), dma((jobs, parts)), dma((2, parts)), dma((jobs, parts)),
+        pltpu.SemaphoreType.REGULAR((jobs,)), pltpu.SemaphoreType.REGULAR((jobs,)),
+        dma((jobs + 4,)), dma((4 + jobs,)),
+    ]
+    shape = jax.ShapeDtypeStruct
+    return pl.pallas_call(
+        partial(layer_kernel, geo),
+        out_shape=(
+            shape(tok.shape, bf16),
+            shape(tok.shape, bf16),
+            shape(tok.shape, f32),
+            shape((2, ff, width), f32),
+            shape((5, 8, width), f32),
+            shape((steps, 8, chunk), f32),
+        ),
+        in_specs=[hbm] * 6 + [vmem] * 3,
+        out_specs=(hbm,) * 4 + (vmem,) * 2,
+        scratch_shapes=scratch,
+        compiler_params=pltpu.CompilerParams(
+            collective_id=1, has_side_effects=True, vmem_limit_bytes=64 * 1024 * 1024 - 256 * 1024),
+        name="encoder_layer",
+    )(tok, cot, w_all, tables[0], tables[1], tables[2], tables[3], vec, bias_in.reshape(steps, 1, chunk))
+
+
+def local_fast(tokens, w_in, b_in, w_out, b_out, gain_one, shift_one, gain_two, shift_two, cotangent):
+    both = ("seq", "batch")
+    parts = lax.axis_size("seq")
+    width = tokens.shape[2]
+    shard = w_in.shape[1]
+    w_all = lax.all_gather(jnp.stack([w_in.T, w_out]), both, axis=1, tiled=True)
+    vectors = jnp.concatenate([b_in, gain_one, shift_one, gain_two, shift_two, b_out])
+    vectors = lax.all_gather(vectors, both, axis=0, tiled=False).astype(f32)
+    bias_in = vectors[:, :shard].reshape(-1)
+    vec = vectors[:, shard:].reshape(vectors.shape[0], 5, -1)
+    vec = jnp.moveaxis(vec, 1, 0).reshape(5, width)
+    vec = jnp.concatenate([vec, jnp.zeros((3, width), f32)], axis=0)
+    out, gtok, _, dw, small, bsum = layer_call(tokens, cotangent, w_all, vec, bias_in, parts)
+    dw = lax.psum_scatter(dw, both, scatter_dimension=1, tiled=True)
+    devices = vectors.shape[0]
+    small = small.sum(1).reshape(5, devices, -1)
+    small = jnp.moveaxis(small, 1, 0).reshape(devices, -1)
+    bsum = bsum.sum(1).reshape(devices, -1)
+    rest = lax.psum_scatter(jnp.concatenate([bsum, small], axis=1), both, scatter_dimension=0, tiled=False)
+    grads = rest[shard:].reshape(5, -1)
+    return (out, gtok, dw[0].T, rest[:shard], dw[1], grads[4], grads[0], grads[1], grads[2], grads[3])
 
 
 def hidden_table(extent):
@@ -154,32 +745,45 @@
 
 
 def solution(mesh):
-    return jax.shard_map(
-        local,
-        mesh=mesh,
-        in_specs=(
-            P("batch", "seq", None),
-            P(None, ("seq", "batch")),
-            P(("seq", "batch")),
-            P(("seq", "batch"), None),
-            P(("seq", "batch")),
-            P(("seq", "batch")),
-            P(("seq", "batch")),
-            P(("seq", "batch")),
-            P(("seq", "batch")),
-            P("batch", "seq", None),
-        ),
-        out_specs=(
-            P("batch", "seq", None),
-            P("batch", "seq", None),
-            P(None, ("seq", "batch")),
-            P(("seq", "batch")),
-            P(("seq", "batch"), None),
-            P(("seq", "batch")),
-            P(("seq", "batch")),
-            P(("seq", "batch")),
-            P(("seq", "batch")),
-            P(("seq", "batch")),
-        ),
-        check_vma=False,
-    )
+    every = P(("seq", "batch"))
+
+    def whole(tokens, w_in, *rest):
+        parts = mesh.shape["seq"]
+        fits = (
+            parts == 8
+            and tokens.shape[1] == 512 * parts
+            and tokens.shape[2] % (32 * parts) == 0
+            and w_in.shape[1] % (3 * 128) == 0
+            and tokens.shape[0] == 4 * mesh.shape["batch"]
+        )
+        return jax.shard_map(
+            local_fast if fits else local,
+            mesh=mesh,
+            in_specs=(
+                P("batch", "seq", None),
+                P(None, ("seq", "batch")),
+                every,
+                P(("seq", "batch"), None),
+                every,
+                every,
+                every,
+                every,
+                every,
+                P("batch", "seq", None),
+            ),
+            out_specs=(
+                P("batch", "seq", None),
+                P("batch", "seq", None),
+                P(None, ("seq", "batch")),
+                every,
+                P(("seq", "batch"), None),
+                every,
+                every,
+                every,
+                every,
+                every,
+            ),
+            check_vma=False,
+        )(tokens, w_in, *rest)
+
+    return whole

time: 1010 us -> 479 us (0.47)
  other arithmetic: 332 us -> 1.82 us
  matrix products: 224 us -> 0 us
  waiting for transfers between devices: 29.9 us -> 200 us
  Pallas kernels: 0 us -> 163 us
  local copies, waits for them, and re-layouts: 155 us -> 15.4 us
  blocking collectives: 220 us -> 84.3 us
  starting transfers between devices: 19.5 us -> 0.08 us
    another operation x9 -> x1, other arithmetic: 274 us -> 1.72 us  [local_fast(): w_all = lax.all_gather(jnp.stack([w_in.T, w_out]), both, axis=1, tiled=True)]
    dot_general x10 -> x0, matrix products: 224 us -> none  [the longest x1 35.6 us: local(): jnp.einsum('plm,bmpc->blc', s_table, lax.all_to_all(spectra, 'seq', split...]
    pallas_call x0 -> x1, Pallas kernels: none -> 163 us  [layer_call(): pl.pallas_call(partial(layer_kernel, geo), out_shape=(shape(tok.shape, bf...]
    reduce_scatter x2 -> x1, waiting for transfers between devices: 0.01 us -> 161 us  [local_fast(): dw = lax.psum_scatter(dw, both, scatter_dimension=1, tiled=True)]
    unnamed x2, blocking collectives: 220 us -> 84.3 us
    convert_element_type x5 -> x1, local copies, waits for them, and re-layouts: 50 us -> 0.1 us  [local_fast(): vectors = lax.all_gather(vectors, both, axis=0, tiled=False).astype(f32)]
    all_to_all x5 -> x0, local copies, waits for them, and re-layouts: 47.7 us -> none  [the longest x1 22 us: local(): lax.all_to_all(spec_grad, 'seq', split_axis=1, concat_axis=3, tiled=True)]
    all_gather x2 -> x1, waiting for transfers between devices: 0.01 us -> 38.8 us  [local_fast(): w_all = lax.all_gather(jnp.stack([w_in.T, w_out]), both, axis=1, tiled=True)]
  transfers between devices with their start and end apart: 8 -> 2, of which waited for: 1 -> 2; matrix products, arithmetic and copies ran while one was open for 64% -> 2% of each run, Pallas kernels for 0% -> 0%
where the time goes in v1:
time: 479 us
  waiting for transfers between devices  200 us (42%)
  Pallas kernels  163 us (34%)
  blocking collectives  84.3 us (18%)
  local copies, waits for them, and re-layouts  15.4 us (3%)
  between operations  14.2 us (3%)
    pallas_call x1, Pallas kernels, layer_call(): pl.pallas_call(partial(layer_kernel, geo), out_shape=(shape(tok.shape, bf...  163 us
    reduce_scatter x1, waiting for transfers between devices, local_fast(): dw = lax.psum_scatter(dw, both, scatter_dimension=1, tiled=True)  161 us
    unnamed x2, blocking collectives  84.3 us
    all_gather x1, waiting for transfers between devices, local_fast(): w_all = lax.all_gather(jnp.stack([w_in.T, w_out]), both, axis=1, tiled=True)  38.8 us
  transfers between devices with their start and end apart: 2, of which 2 were waited for; matrix products, arithmetic and copies ran while one was open for 2% of the time, Pallas kernels for 0%

profile of v1, /device:TPU:0, one launch (start us, length us, event | category | flops | bytes accessed | tf_op | source)
XLA Modules:
  0.0 478.5 jit_solution(4814443088403879377)
XLA Ops:
  7.2 0.0 all-gather.3.cloned.1.call-start
  7.2 1.7 pad_maximum_fusion
  8.9 0.0 all-gather.3.cloned.1.call-update
  9.0 0.0 reduce-scatter.3.cloned.1.call-start
  9.0 4.1 concatenate.9
  13.1 0.2 dynamic-update-slice
  13.4 42.8 %all-reduce.1 = bf16[6912]{0:T(1024)(128)(2,1)S(1)} all-reduce(bf16[6912]{0:T(1024)(128)(2,1)S(1)} %dynamic-update-slice), channel_id=2, replica_groups=mesh['seq'=8,'batch'=4] {'seq','batch'}, use_global_device_ids=true, to_apply=%add.1 | all-reduce | flops 6912 | bytes 27648
  56.2 0.1 reshape.55
  56.3 0.1 slice.56
  56.3 0.1 copy.37
  56.4 0.1 copy.38
  56.5 0.1 reshape.50
  56.6 0.7 reshape_reshape.3.bias_in
  57.3 0.6 concatenate.10.vec
  57.9 38.8 %all-gather.3.cloned.1.call-done.w_all = bf16[2,3072,768]{2,1,0:T(8,128)(2,1)} async-done(((bf16[2,96,768]{2,1,0:T(8,128)(2,1)}), bf16[2,3072,768]{2,1,0:T(8,128)(2,1)}) %all-gather.3.cloned.1.call-update) | async-done | bytes 9437200 | tf_op jit(solution)/shard_map/all_gather | solution.py:585
  96.7 162.9 %encoder_layer.1 = (bf16[4,512,768]{2,1,0:T(8,128)(2,1)}, bf16[4,512,768]{2,1,0:T(8,128)(2,1)}, f32[4,512,768]{2,1,0:T(8,128)}, f32[2,3072,768]{2,1,0:T(8,128)},...) custom-call(bf16[4,512,768]{2,1,0:T(8,128)(2,1)} %tok.1, bf16[4,512,768]{2,1,0:T(8,128)(2,1)} %cot.1, ...), custom_call_target="tpu_custom_call" | custom-call | tf_op jit(solution)/shard_map/encoder_layer/pallas_call | solution.py:561
  259.6 0.0 copy-start.2
  259.7 0.0 copy-start.3
  259.7 0.0 reduce-scatter.3.cloned.1.call-update
  259.7 0.8 copy-done.2
  260.6 0.1 reshape.52
  260.7 0.1 copy.39
  260.8 0.1 reshape.51
  260.9 0.1 copy.40
  261.0 41.5 %all-reduce.2 = f32[32,216]{0,1:T(8,128)S(1)} all-reduce(f32[32,216]{0,1:T(8,128)S(1)} %pad_maximum_fusion.1), channel_id=4, replica_groups=mesh['seq'=8,'batch'=4] {'seq','batch'}, use_global_device_ids=true, to_apply=%region_3.0.clone | all-reduce | flops 6912 | bytes 55296
  302.5 0.7 dynamic-slice_reduce_fusion
  303.2 0.8 dynamic-slice_reduce_fusion.1
  304.0 161.1 %reduce-scatter.3.cloned.1.call-done = f32[2,96,768]{2,1,0:T(8,128)} async-done(((f32[2,3072,768]{2,1,0:T(8,128)}), f32[2,96,768]{2,1,0:T(8,128)}) %reduce-scatter.3.cloned.1.call-update) | async-done | bytes 589840 | tf_op jit(solution)/shard_map/reduce_scatter | solution.py:593
  465.1 1.9 slice_bitcast_fusion
  467.0 1.7 copy.46
  468.7 1.4 copy-done
  470.0 1.7 copy.47
  (9 shorter events, 0.1 us)
Async XLA Ops:
  7.2 89.6 %all-gather.3.cloned.1.call-start = ((), (), s32[]{:S(2)}) async-start(), calls=%async_computation.1 | async-start | bytes 9732096 | tf_op jit(solution)/shard_map/all_gather | solution.py:585
  9.0 456.1 %reduce-scatter.3.cloned.1.call-start = ((), (), s32[]{:S(2)}) async-start(), calls=%async_computation.2 | async-start | bytes 19464192 | tf_op jit(solution)/shard_map/reduce_scatter | solution.py:593
  259.6 0.9 copy-start.2
  259.7 1.1 copy-start.3
  259.7 207.3 %copy-start.1 = (bf16[4,512,768]{2,1,0:T(8,128)(2,1)S(1)}, bf16[4,512,768]{2,1,0:T(8,128)(2,1)}, u32[]{:S(2)}) copy-start(bf16[4,512,768]{2,1,0:T(8,128)(2,1)} %get-tuple-element.37) | copy-start | bytes 9437188
  467.0 3.0 copy-start
Sparse Core Ops, SparseCore 0:
  11.7 85.0 all-gather.2
  259.8 205.2 reduce-scatter.2

commit v2 on v1

--- a/solution.py
+++ b/solution.py
@@ -281,11 +281,13 @@
 
 
 def layer_kernel(geo, tok, cot, w_all, hp_all, wd_all, cp_all, tw, vec, bias_in,
-                 out, gtok, grow, dw_all, small, bsum,
+                 out, gtok, grow, dw_own, small,
                  tokv, cotv, outv, w, hp, wd, cp, dw, send1, recv1, send2, recv2, t_ref, o_ref,
-                 nbuf, sbuf, alow, hid, slope, acc, glow, sums,
-                 ss1, rs1, ss2, rs2, free1, free2, load, io):
-    parts, pairs, span, width, jobs, chunk, rows_step = geo
+                 nbuf, sbuf, alow, hid, slope, acc, glow, sums, bsum, rz, sv, rv,
+                 ss1, rs1, ss2, rs2, free1, free2, load, io,
+                 s_core, r_core, s_first, r_first, s_next, r_next, s_z, r_z, s_vec, r_vec, ready):
+    parts, pairs, span, width, jobs, chunk, rows_step, planes = geo
+    shard = dw.shape[1] // (parts * planes)
     me = lax.axis_index("seq")
     plane = lax.axis_index("batch")
 
@@ -295,11 +297,20 @@
     def load_of(k):
         if k < jobs:
             return pltpu.make_async_copy(tok.at[k], tokv.at[k], load.at[k])
-        a, b = ((hp_all, hp), (wd_all, wd), (cp_all, cp), (w_all, w))[k - jobs]
+        a, b = ((hp_all, hp), (wd_all, wd), (cp_all, cp))[k - jobs]
         return pltpu.make_async_copy(a, b, load.at[k])
 
-    for k in (jobs, 0, 1, jobs + 1, 2, 3, jobs + 2, jobs + 3):
+    for k in (jobs, 0, 1, jobs + 1, 2, 3, jobs + 2):
         load_of(k).start()
+
+    def weights(o, carry):
+        for m in range(2):
+            pltpu.make_async_copy(
+                w_all.at[o, pl.ds(m * shard, shard)], w.at[m, pl.ds(pl.multiple_of(o * shard, shard), shard)],
+                load.at[jobs + 3]).start()
+        return carry
+
+    lax.fori_loop(0, parts * planes, weights, 0)
 
     barrier = pltpu.get_barrier_semaphore()
 
@@ -307,8 +318,13 @@
         pl.semaphore_signal(barrier, inc=1, device_id=(peer(d), plane), device_id_type=MESH)
         return carry
 
+    def greet_z(d, carry):
+        pl.semaphore_signal(barrier, inc=1, device_id=(me, lax.rem(plane + d, planes)), device_id_type=MESH)
+        return carry
+
     lax.fori_loop(1, parts, greet, 0)
-    pl.semaphore_wait(barrier, parts - 1)
+    lax.fori_loop(1, planes, greet_z, 0)
+    pl.semaphore_wait(barrier, parts - 1 + planes - 1)
 
     def remote(send, recv, ss, rs, k, d):
         p = peer(d)
@@ -421,7 +437,7 @@
         return carry
 
     lax.fori_loop(0, 2, fill, 0)
-    load_of(jobs + 3).wait()
+    pltpu.make_async_copy(w, w, load.at[jobs + 3]).wait()
 
     def out_copy(i):
         return pltpu.make_async_copy(outv, out.at[i], io.at[0])
@@ -473,9 +489,112 @@
         return carry
 
     lax.fori_loop(0, jobs, main, 0)
-    dw_copy = pltpu.make_async_copy(dw, dw_all, io.at[3])
-    dw_copy.start()
-    small[...] = sums[...]
+
+    core, quad = lax.rem(me, 2), me // 2
+    x, y = lax.rem(quad, 2), quad // 2
+    partner = (me + 1 - 2 * core, plane)
+    x_peer = (me + 2 - 4 * x, plane)
+    y_peer = (me + 4 - 8 * y, plane)
+    quads = parts // 2
+    group = 2 * quads * shard
+
+    def rows_at(start, count=shard):
+        return pl.ds(pl.multiple_of(start, shard), count)
+
+    def target(v):
+        return lax.rem(plane + 1 + v, planes)
+
+    def owned(q, c, v):
+        return rows_at(((2 * q + c) * planes + target(v)) * shard)
+
+    def send(src, dst, s, r, to):
+        return pltpu.make_async_remote_copy(
+            src_ref=src, dst_ref=dst, send_sem=s, recv_sem=r, device_id=to, device_id_type=MESH)
+
+    def core_copy(v):
+        at = rows_at(v * group, group)
+        return send(w.at[0, at], w.at[1, at], s_core.at[v], r_core.at[v], partner)
+
+    def first_copy(v, m):
+        return send(w.at[0, rows_at((planes + v) * quads * shard + 2 * m * shard, 2 * shard)],
+                    w.at[0, rows_at(v * quads * shard + 2 * m * shard, 2 * shard)],
+                    s_first.at[v, m], r_first.at[v, m], (x_peer, y_peer)[m])
+
+    def next_copy(v, m):
+        return send(w.at[1, rows_at((2 * v + m) * shard)], (alow, glow)[m].at[rows_at(v * shard)],
+                    s_next.at[v, m], r_next.at[v, m], (y_peer, x_peer)[m])
+
+    def z_copy(v):
+        return send(w.at[1, rows_at((2 * planes + 2 * v) * shard, 2 * shard)], rz.at[v],
+                    s_z.at[v], r_z.at[v], (me, target(v)))
+
+    def vec_copy(k):
+        to = (partner, x_peer, y_peer)[k] if k < 3 else (me, target(k - 3))
+        return send(sv.at[min(k, 3)], rv.at[k], s_vec.at[k], r_vec.at[k], to)
+
+    def core_step(v, carry):
+        for q in range(quads):
+            for m in range(2):
+                w[0, rows_at(v * group + (2 * q + m) * shard)] = dw[m, owned(q, 1 - core, v)].astype(bf16)
+        core_copy(v).start()
+        return carry
+
+    def first_step(v, carry):
+        core_copy(v).wait_recv()
+        for q in range(quads):
+            for m in range(2):
+                at = owned(q, core, v)
+                dw[m, at] += w[1, rows_at(v * group + (2 * q + m) * shard)].astype(f32)
+        for k in range(2):
+            for m in range(2):
+                q = 2 * k + 1 - x if m == 0 else 2 * (1 - y) + k
+                at = rows_at((planes + v) * quads * shard + (2 * m + k) * shard)
+                w[0, at] = dw[m, owned(q, core, v)].astype(bf16)
+        for m in range(2):
+            first_copy(v, m).start()
+        return carry
+
+    def next_step(v, carry):
+        for m in range(2):
+            first_copy(v, m).wait_recv()
+        for k in range(2):
+            for m in range(2):
+                q = 2 * k + x if m == 0 else 2 * y + k
+                dw[m, owned(q, core, v)] += w[0, rows_at(v * quads * shard + (2 * m + k) * shard)].astype(f32)
+        for m in range(2):
+            q = 2 * (1 - y) + x if m == 0 else 2 * y + 1 - x
+            w[1, rows_at((2 * v + m) * shard)] = dw[m, owned(q, core, v)].astype(bf16)
+            next_copy(v, m).start()
+        return carry
+
+    def z_step(v, carry):
+        for m in range(2):
+            next_copy(v, m).wait_recv()
+            dw[m, owned(quad, core, v)] += (alow, glow)[m][rows_at(v * shard)].astype(f32)
+
+        @pl.when(v < planes - 1)
+        def _():
+            for m in range(2):
+                at = rows_at((2 * planes + 2 * v + m) * shard)
+                w[1, at] = dw[m, owned(quad, core, v)].astype(bf16)
+            z_copy(v).start()
+
+        return carry
+
+    def vec_step(k):
+        if k == 0:
+            sv[0] = jnp.zeros_like(sv[0])
+            for j in range(5):
+                sv[0, j:j + 1] = jnp.sum(sums[j], axis=0, keepdims=True)
+            piece = math.gcd(width, chunk)
+            for f in range(0, bsum.shape[0] * chunk, piece):
+                sv[0, 5 + f // width:6 + f // width, f % width:f % width + piece] = jnp.sum(
+                    bsum[f // chunk, :, f % chunk:f % chunk + piece], axis=0, keepdims=True)
+        else:
+            vec_copy(k - 1).wait_recv()
+            sv[k] = sv[k - 1] + rv[k - 1]
+        for j in ((k,) if k < 3 else range(3, 2 + planes)):
+            vec_copy(j).start()
 
     def gt_copy(i):
         return pltpu.make_async_copy(tokv.at[i], gtok.at[i], io.at[4 + i])
@@ -497,31 +616,82 @@
             pl.semaphore_wait(free2.at[i + 2], parts - 1)
 
         sequence_job(i + 6, before)
-        return carry
-
-    lax.fori_loop(0, 2, drain, 0)
+
+        @pl.when(i == 0)
+        def _():
+            lax.fori_loop(0, planes, first_step, 0)
+
+        return carry
 
     def finish(i, carry):
         final(i + 2)
         wait_sends(*way_back, i + 6)
         wait_sends(*one_way, i + 6)
-        return carry
-
+
+        @pl.when(i == 0)
+        def _():
+            lax.fori_loop(0, planes, z_step, 0)
+
+        return carry
+
+    pl.semaphore_signal(ready.at[0], inc=1, device_id=partner, device_id_type=MESH)
+    pl.semaphore_wait(ready.at[0], 1)
+    lax.fori_loop(0, planes, core_step, 0)
+    vec_step(0)
+
+    def core_sent(v, carry):
+        core_copy(v).wait_send()
+        return carry
+
+    lax.fori_loop(0, planes, core_sent, 0)
+    pl.semaphore_signal(ready.at[1], inc=1, device_id=x_peer, device_id_type=MESH)
+    pl.semaphore_signal(ready.at[2], inc=1, device_id=y_peer, device_id_type=MESH)
+    vec_step(1)
+    pl.semaphore_wait(ready.at[1], 1)
+    pl.semaphore_wait(ready.at[2], 1)
+    lax.fori_loop(0, 2, drain, 0)
+    vec_step(2)
+    lax.fori_loop(0, planes, next_step, 0)
+    vec_step(3)
     lax.fori_loop(0, 2, finish, 0)
+    own_rows = owned(quad, core, planes - 1)
+    for m in range(2):
+        dw_own[m] = dw[m, own_rows]
+    for v in range(planes - 1):
+        z_copy(v).wait_recv()
+        for m in range(2):
+            dw_own[m] += rz[v, m * shard:(m + 1) * shard].astype(f32)
+    total = sv[3]
+    for k in range(3, 2 + planes):
+        vec_copy(k).wait_recv()
+        total = total + rv[k]
+    small[...] = total
+
+    def sent(v, carry):
+        for m in range(2):
+            first_copy(v, m).wait_send()
+            next_copy(v, m).wait_send()
+        return carry
+
+    lax.fori_loop(0, planes, sent, 0)
+    for v in range(planes - 1):
+        z_copy(v).wait_send()
+    for k in range(2 + planes):
+        vec_copy(k).wait_send()
     out_copy(jobs - 1).wait()
-    dw_copy.wait()
     for i in range(jobs):
         gt_copy(i).wait()
 
 
-def layer_call(tok, cot, w_all, vec, bias_in, parts):
+def layer_call(tok, cot, w_all, vec, bias_in, parts, planes):
     jobs, span, width = tok.shape
-    ff = w_all.shape[1]
+    ff = bias_in.size
+    shard = ff // (parts * planes)
     pairs = width // 2 // parts
     chunk, rows_step = ff // 3, span // 2
     steps = ff // chunk
     length = span * parts
-    geo = (parts, pairs, span, width, jobs, chunk, rows_step)
+    geo = (parts, pairs, span, width, jobs, chunk, rows_step, planes)
     tables = (
         jnp.asarray(packed_hidden(width, parts)),
         jnp.asarray(inner_table(span, length)),
@@ -553,9 +723,16 @@
         pltpu.VMEM((span, width), f32),
         pltpu.VMEM((span, width), bf16),
         pltpu.VMEM((5, 8, width), f32),
+        pltpu.VMEM((steps, 8, chunk), f32),
+        pltpu.VMEM((planes - 1, 2 * shard, width), bf16),
+        pltpu.VMEM((4, 16, width), f32),
+        pltpu.VMEM((2 + planes, 16, width), f32),
         dma((2, parts)), dma((jobs, parts)), dma((2, parts)), dma((jobs, parts)),
         pltpu.SemaphoreType.REGULAR((jobs,)), pltpu.SemaphoreType.REGULAR((jobs,)),
         dma((jobs + 4,)), dma((4 + jobs,)),
+        dma((planes,)), dma((planes,)), dma((planes, 2)), dma((planes, 2)), dma((planes, 2)), dma((planes, 2)),
+        dma((planes - 1,)), dma((planes - 1,)), dma((2 + planes,)), dma((2 + planes,)),
+        pltpu.SemaphoreType.REGULAR((3,)),
     ]
     shape = jax.ShapeDtypeStruct
     return pl.pallas_call(
@@ -564,12 +741,11 @@
             shape(tok.shape, bf16),
             shape(tok.shape, bf16),
             shape(tok.shape, f32),
-            shape((2, ff, width), f32),
-            shape((5, 8, width), f32),
-            shape((steps, 8, chunk), f32),
+            shape((2, shard, width), f32),
+            shape((16, width), f32),
         ),
         in_specs=[hbm] * 6 + [vmem] * 3,
-        out_specs=(hbm,) * 4 + (vmem,) * 2,
+        out_specs=(hbm,) * 3 + (vmem,) * 2,
         scratch_shapes=scratch,
         compiler_params=pltpu.CompilerParams(
             collective_id=1, has_side_effects=True, vmem_limit_bytes=64 * 1024 * 1024 - 256 * 1024),
@@ -582,22 +758,22 @@
     parts = lax.axis_size("seq")
     width = tokens.shape[2]
     shard = w_in.shape[1]
-    w_all = lax.all_gather(jnp.stack([w_in.T, w_out]), both, axis=1, tiled=True)
-    vectors = jnp.concatenate([b_in, gain_one, shift_one, gain_two, shift_two, b_out])
-    vectors = lax.all_gather(vectors, both, axis=0, tiled=False).astype(f32)
+    planes = lax.axis_size("batch")
+    pad = 16 * width - shard - 5 * b_out.shape[0]
+    vectors = jnp.concatenate([b_in, gain_one, shift_one, gain_two, shift_two, b_out, jnp.zeros((pad,), bf16)])
+    packed = jnp.concatenate([w_in.T, w_out, vectors.reshape(16, width)], axis=0)
+    w_all = lax.all_gather(packed, both, axis=0, tiled=False)
+    vectors = w_all[:, 2 * shard].astype(f32)
     bias_in = vectors[:, :shard].reshape(-1)
-    vec = vectors[:, shard:].reshape(vectors.shape[0], 5, -1)
+    vec = vectors[:, shard:shard + 5 * b_out.shape[0]].reshape(vectors.shape[0], 5, -1)
     vec = jnp.moveaxis(vec, 1, 0).reshape(5, width)
     vec = jnp.concatenate([vec, jnp.zeros((3, width), f32)], axis=0)
-    out, gtok, _, dw, small, bsum = layer_call(tokens, cotangent, w_all, vec, bias_in, parts)
-    dw = lax.psum_scatter(dw, both, scatter_dimension=1, tiled=True)
-    devices = vectors.shape[0]
-    small = small.sum(1).reshape(5, devices, -1)
-    small = jnp.moveaxis(small, 1, 0).reshape(devices, -1)
-    bsum = bsum.sum(1).reshape(devices, -1)
-    rest = lax.psum_scatter(jnp.concatenate([bsum, small], axis=1), both, scatter_dimension=0, tiled=False)
-    grads = rest[shard:].reshape(5, -1)
-    return (out, gtok, dw[0].T, rest[:shard], dw[1], grads[4], grads[0], grads[1], grads[2], grads[3])
+    out, gtok, _, dw, small = layer_call(tokens, cotangent, w_all, vec, bias_in, parts, planes)
+    owner = lax.axis_index("seq") * planes + lax.axis_index("batch")
+    grad_b_in = lax.dynamic_slice(small[5:9].reshape(-1), (owner * shard,), (shard,))
+    part = b_out.shape[0]
+    rest = lax.dynamic_slice(small[:5], (0, owner * part), (5, part))
+    return (out, gtok, dw[0].T, grad_b_in, dw[1], rest[4], rest[0], rest[1], rest[2], rest[3])
 
 
 def hidden_table(extent):

time: 479 us -> 347 us (0.72)
  waiting for transfers between devices: 200 us -> 88.4 us
  blocking collectives: 84.3 us -> 0 us
  Pallas kernels: 163 us -> 220 us
    reduce_scatter x1 -> x0, waiting for transfers between devices: 161 us -> none  [local_fast(): dw = lax.psum_scatter(dw, both, scatter_dimension=1, tiled=True)]
    unnamed x2 -> x0, blocking collectives: 84.3 us -> none
    pallas_call x1, Pallas kernels: 163 us -> 220 us  [layer_call(): pl.pallas_call(partial(layer_kernel, geo), out_shape=(shape(tok.shape, bf...]
    all_gather x1, waiting for transfers between devices: 38.8 us -> 88.4 us  [local_fast(): w_all = lax.all_gather(packed, both, axis=0, tiled=False)]
  transfers between devices with their start and end apart: 2 -> 1, of which waited for: 2 -> 1; matrix products, arithmetic and copies ran while one was open for 2% -> 0% of each run, Pallas kernels for 0% -> 0%
where the time goes in v2:
time: 347 us; the launch traced here: 342 us
  Pallas kernels  220 us (63%)
  waiting for transfers between devices  88.4 us (25%)
  local copies, waits for them, and re-layouts  16 us (5%)
  between operations  14.1 us (4%)
    pallas_call x1, Pallas kernels, layer_call(): pl.pallas_call(partial(layer_kernel, geo), out_shape=(shape(tok.shape, bf...  220 us
    all_gather x1, waiting for transfers between devices, local_fast(): w_all = lax.all_gather(packed, both, axis=0, tiled=False)  88.4 us
  transfers between devices with their start and end apart: 1, of which 1 were waited for; matrix products, arithmetic and copies ran while one was open for 0% of the time, Pallas kernels for 0%

profile of v2, /device:TPU:0, one launch (start us, length us, event | category | flops | bytes accessed | tf_op | source)
XLA Modules:
  0.0 341.7 jit_solution(5165606963899485698)
XLA Ops:
  7.2 0.0 all-gather.3.cloned.1.call-start
  7.2 4.1 %concatenate.9 = bf16[12288]{0:T(1024)(128)(2,1)S(1)} concatenate(bf16[96]{0:T(256)(128)(2,1)} %param.16, bf16[24]{0:T(256)(128)(2,1)} %param.19, bf16[24]{0:T(256)(128)(2,1)} %param.20, bf16[24]{0:T(256)(128)(2,1)} %param.21, bf16[24]{0:T(256)(128)(2,1)} %param.22, bf16[24]{0:T(256)(128)(2,1)} %param.18, bf16[12072]{0:T(1024)(128)(2,1)S(1)} %broadcast_in_dim.4), dimensions={0} | concatenate | bytes 49152 | tf_op jit(solution)/shard_map/concatenate | solution.py:763
  11.4 1.7 pad_maximum_fusion
  13.1 0.0 all-gather.3.cloned.1.call-update
  13.2 88.4 %all-gather.3.cloned.1.call-done = bf16[6656,768]{1,0:T(8,128)(2,1)} async-done(((bf16[208,768]{1,0:T(8,128)(2,1)}), bf16[6656,768]{1,0:T(8,128)(2,1)}) %all-gather.3.cloned.1.call-update) | async-done | bytes 10223632 | tf_op jit(solution)/shard_map/all_gather | solution.py:765
  101.6 1.0 slice_convert_fusion
  102.6 0.1 slice.49
  102.7 0.1 copy.25
  102.8 0.1 copy.26
  102.9 0.1 reshape.36
  103.0 0.7 reshape_reshape.3.bias_in
  103.7 0.6 concatenate.11.vec
  104.3 220.4 %encoder_layer.1 = (bf16[4,512,768]{2,1,0:T(8,128)(2,1)}, bf16[4,512,768]{2,1,0:T(8,128)(2,1)}, f32[4,512,768]{2,1,0:T(8,128)}, f32[2,96,768]{2,1,0:T(8,128)}, f32[16,768]{1,0:T(8,128)}) custom-call(bf16[4,512,768]{2,1,0:T(8,128)(2,1)} %tok.1, bf16[4,512,768]{2,1,0:T(8,128)(2,1)} %cot.1, bf16[32,208,768]{2,1,0:T(8,128)(2,1)} %bitcast.25, ...), custom_call_target="tpu_custom_call" | custom-call | tf_op jit(solution)/shard_map/encoder_layer/pallas_call | solution.py:738
  324.7 0.8 slice.40
  325.5 0.7 slice.42
  326.2 1.9 slice_bitcast_fusion
  328.1 0.1 constant_dynamic-slice_fusion
  328.2 0.5 slice_bitcast_fusion.2
  328.7 0.6 dynamic_slice.6
  329.3 0.0 copy-start
  329.3 3.9 %copy.32 = bf16[4,512,768]{2,1,0:T(8,128)(2,1)} copy(bf16[4,512,768]{2,1,0:T(8,128)(2,1)} %get-tuple-element.35) | data formatting | bytes 6291456
  333.2 0.0 copy-done
  333.2 1.7 copy.33
  (5 shorter events, 0.1 us)
Async XLA Ops:
  7.2 94.4 %all-gather.3.cloned.1.call-start = ((), (), s32[]{:S(2)}) async-start(), calls=%async_computation | async-start | bytes 10543104 | tf_op jit(solution)/shard_map/all_gather | solution.py:765
  329.3 3.9 %copy-start = (bf16[4,512,768]{2,1,0:T(8,128)(2,1)S(1)}, bf16[4,512,768]{2,1,0:T(8,128)(2,1)}, u32[]{:S(2)}) copy-start(bf16[4,512,768]{2,1,0:T(8,128)(2,1)} %get-tuple-element.36) | copy-start | bytes 9437188
Sparse Core Ops, SparseCore 0:
  13.3 88.2 all-gather.2

commit v3 on v2

--- a/solution.py
+++ b/solution.py
@@ -130,9 +130,9 @@
     lax.fori_loop(0, span // 128, tile, 0)
 
 
-def spread_step(o_ref, put, me, parts, pairs, span, u):
+def spread_step(o_ref, put, me, parts, pairs, u, half):
     count = 2 * parts * pairs
-    lanes = pl.ds(pl.multiple_of(u * 128, 128), 128)
+    lanes = pl.ds(pl.multiple_of((u - half * parts // 4) * 128, 128), 128)
     low = lax.broadcasted_iota(jnp.int32, (16, 128), 1) < 64
     row = lax.broadcasted_iota(jnp.int32, (16, 128), 0)
     special = (row == 0) & (jnp.zeros((16, 128), jnp.int32) + me == 0)
@@ -189,7 +189,7 @@
     return value, slope
 
 
-def ffn_forward(x_get, nbuf, sbuf, alow, hid, slope, acc, w, vec, bias_in, chunk, rows_step):
+def ffn_forward(x_get, nbuf, sbuf, alow, hid, slope, acc, weight, vec, bias_in, rows_step):
     rows = nbuf.shape[1]
 
     def first(r, carry):
@@ -206,13 +206,12 @@
     lax.fori_loop(0, rows // rows_step, first, 0)
 
     def step(c, carry):
-        at = pl.ds(pl.multiple_of(c * chunk, chunk), chunk)
-        pre = dot_nt(alow[...], w[0, at, :]) + bias_in[c]
+        pre = dot_nt(alow[...], weight(0, c)) + bias_in[c]
         value, back = gelu_pair(pre)
         low = value.astype(bf16)
         hid[c] = low
         slope[c] = back.astype(bf16)
-        part = dot_nn(low, w[1, at, :])
+        part = dot_nn(low, weight(1, c))
 
         @pl.when(c == 0)
         def _():
@@ -251,18 +250,18 @@
     lax.fori_loop(0, rows // rows_step, second, 0)
 
 
-def ffn_backward(nbuf, sbuf, alow, hid, slope, acc, glow, w, dw, bsum, vec, sums, chunk, rows_step, put):
+def ffn_backward(nbuf, sbuf, alow, hid, slope, acc, glow, weight, dw, bsum, vec, sums, chunk, rows_step, put):
     rows = nbuf.shape[1]
 
     def step(c, carry):
         at = pl.ds(pl.multiple_of(c * chunk, chunk), chunk)
-        gh = dot_nt(glow[...], w[1, at, :])
+        gh = dot_nt(glow[...], weight(1, c))
         pre32 = gh * slope[c].astype(f32)
         gpre = pre32.astype(bf16)
         bsum[c] += fold(gpre.astype(f32))
         dw[1, at, :] += dot_tn(hid[c], glow[...])
         dw[0, at, :] += dot_tn(gpre, alow[...])
-        acc[...] += dot_nn(gpre, w[0, at, :])
+        acc[...] += dot_nn(gpre, weight(0, c))
         return carry
 
     lax.fori_loop(0, hid.shape[0], step, 0)
@@ -280,13 +279,14 @@
     lax.fori_loop(0, rows // rows_step, last, 0)
 
 
-def layer_kernel(geo, tok, cot, w_all, hp_all, wd_all, cp_all, tw, vec, bias_in,
+def layer_kernel(geo, tok, cot, win_own, wout_own, vec_own, hp_all, wd_all, cp_all, tw,
                  out, gtok, grow, dw_own, small,
-                 tokv, cotv, outv, w, hp, wd, cp, dw, send1, recv1, send2, recv2, t_ref, o_ref,
-                 nbuf, sbuf, alow, hid, slope, acc, glow, sums, bsum, rz, sv, rv,
+                 tokv, cotv, outv, w0, w1, hp, wd, cp, dw, send1, recv1, send2, recv2, t_ref, o_ref,
+                 nbuf, sbuf, alow, hid, slope, acc, glow, sums, bsum, rz, sv, rv, vec, bias_in,
                  ss1, rs1, ss2, rs2, free1, free2, load, io,
-                 s_core, r_core, s_first, r_first, s_next, r_next, s_z, r_z, s_vec, r_vec, ready):
-    parts, pairs, span, width, jobs, chunk, rows_step, planes = geo
+                 s_core, r_core, s_first, r_first, s_next, r_next, s_z, r_z, s_vec, r_vec, ready,
+                 s_spread, r_spread, s_relay, r_relay, s_pair, r_pair):
+    parts, pairs, span, width, jobs, slots, chunk, rows_step, planes = geo
     shard = dw.shape[1] // (parts * planes)
     me = lax.axis_index("seq")
     plane = lax.axis_index("batch")
@@ -303,14 +303,22 @@
     for k in (jobs, 0, 1, jobs + 1, 2, 3, jobs + 2):
         load_of(k).start()
 
-    def weights(o, carry):
-        for m in range(2):
-            pltpu.make_async_copy(
-                w_all.at[o, pl.ds(m * shard, shard)], w.at[m, pl.ds(pl.multiple_of(o * shard, shard), shard)],
-                load.at[jobs + 3]).start()
-        return carry
-
-    lax.fori_loop(0, parts * planes, weights, 0)
+    core, quad = lax.rem(me, 2), me // 2
+    quads = parts // 2
+    partner = (me + 1 - 2 * core, plane)
+    last = planes - 1
+
+    def send(src, dst, s, r, to):
+        return pltpu.make_async_remote_copy(
+            src_ref=src, dst_ref=dst, send_sem=s, recv_sem=r, device_id=to, device_id_type=MESH)
+
+    own_loads = (
+        pltpu.make_async_copy(win_own, w0.at[quad, core, plane, pl.ds(0, shard)], load.at[jobs + 3]),
+        pltpu.make_async_copy(vec_own, w0.at[quad, core, plane, pl.ds(shard, 16)], load.at[jobs + 4]),
+        pltpu.make_async_copy(wout_own, w1.at[quad, core, plane], load.at[jobs + 5]),
+    )
+    for copy in own_loads:
+        copy.start()
 
     barrier = pltpu.get_barrier_semaphore()
 
@@ -329,13 +337,13 @@
     def remote(send, recv, ss, rs, k, d):
         p = peer(d)
         return pltpu.make_async_remote_copy(
-            src_ref=send.at[lax.rem(k, 2), p], dst_ref=recv.at[lax.rem(k, jobs), me],
-            send_sem=ss.at[lax.rem(k, 2), d], recv_sem=rs.at[lax.rem(k, jobs), d],
+            src_ref=send.at[lax.rem(k, 2), p], dst_ref=recv.at[lax.rem(k, slots), me],
+            send_sem=ss.at[lax.rem(k, 2), d], recv_sem=rs.at[lax.rem(k, slots), d],
             device_id=(p, plane), device_id_type=MESH)
 
     def own(send, recv, rs, k):
         return pltpu.make_async_copy(
-            send.at[lax.rem(k, 2), me], recv.at[lax.rem(k, jobs), me], rs.at[lax.rem(k, jobs), 0])
+            send.at[lax.rem(k, 2), me], recv.at[lax.rem(k, slots), me], rs.at[lax.rem(k, slots), 0])
 
     def wait_sends(send, recv, ss, rs, k):
         def one(d, carry):
@@ -349,7 +357,7 @@
 
         def one(d, carry):
             source = lax.rem(me + parts - d, parts)
-            slot = lax.rem(k, jobs)
+            slot = lax.rem(k, slots)
             pltpu.make_async_remote_copy(
                 src_ref=send.at[0, 0], dst_ref=recv.at[slot, source],
                 send_sem=ss.at[0, d], recv_sem=rs.at[slot, d],
@@ -358,12 +366,143 @@
 
         lax.fori_loop(1, parts, one, 0)
 
-    def tell(sem, slot):
+    def tell(sem, k):
         def one(d, carry):
-            pl.semaphore_signal(sem.at[slot], inc=1, device_id=(peer(d), plane), device_id_type=MESH)
+            pl.semaphore_signal(sem.at[lax.rem(k, slots)], inc=1, device_id=(peer(d), plane), device_id_type=MESH)
             return carry
 
         lax.fori_loop(1, parts, one, 0)
+
+    def in_plane(d):
+        return 2 * lax.rem(quad + d, quads) + core
+
+    def along(d):
+        return lax.rem(plane + d, planes)
+
+    def spread_z(d):
+        block = w0.at[quad, core, plane]
+        return send(block, block, s_spread.at[0, d], r_spread.at[0, d], (me, along(d)))
+
+    def spread_out(d):
+        block = w1.at[quad, core, plane]
+        return send(block, block, s_spread.at[1, d], r_spread.at[1, d], (in_plane(d), plane))
+
+    def spread_in(d):
+        block = w0.at[quad, core]
+        return send(block, block, s_spread.at[2, d], r_spread.at[2, d], (in_plane(d), plane))
+
+    def relay(origin, up):
+        block = w1.at[:, core, origin]
+        return send(block, block, s_relay.at[up, origin], r_relay.at[origin], (me, plane + 2 * up - 1))
+
+    def pair_in(q):
+        block = w0.at[q, core]
+        return send(block, block, s_pair.at[0, q], r_pair.at[0, q], partner)
+
+    def pair_out(origin):
+        block = w1.at[:, core, origin]
+        return send(block, block, s_pair.at[1, origin], r_pair.at[1, origin], partner)
+
+    def relay_step(j):
+        below, above = plane - 1 - j, plane + 1 + j
+
+        @pl.when(below >= 0)
+        def _():
+            relay(below, 1).wait_recv()
+
+            @pl.when(plane < last)
+            def _():
+                relay(below, 1).start()
+
+            pair_out(below).start()
+
+        @pl.when(above <= last)
+        def _():
+            relay(above, 0).wait_recv()
+
+            @pl.when(plane > 0)
+            def _():
+                relay(above, 0).start()
+
+            pair_out(above).start()
+
+    def gather_start():
+        for copy in own_loads:
+            copy.wait()
+        for d in range(1, planes):
+            spread_z(d).start()
+        for d in range(1, quads):
+            spread_out(d).start()
+
+    def gather_out():
+        for d in range(1, quads):
+            spread_out(d).wait_recv()
+
+        @pl.when(plane < last)
+        def _():
+            relay(plane, 1).start()
+
+        @pl.when(plane > 0)
+        def _():
+            relay(plane, 0).start()
+
+        pair_out(plane).start()
+
+    def gather_in():
+        for d in range(1, planes):
+            spread_z(d).wait_recv()
+        for d in range(1, quads):
+            spread_in(d).start()
+        pair_in(quad).start()
+
+    def gather_pass():
+        for d in range(1, quads):
+            spread_in(d).wait_recv()
+            pair_in(lax.rem(quad + quads - d, quads)).start()
+
+    def gather_end():
+        for q in range(quads):
+            pair_in(q).wait_recv()
+        for origin in range(planes):
+            pair_out(origin).wait_recv()
+
+        def one(o, carry):
+            rest = lax.rem(o, 2 * planes)
+            block = w0[o // (2 * planes), rest // planes, lax.rem(rest, planes), shard:shard + 16, :]
+            return carry + block.astype(f32)
+
+        total = lax.fori_loop(0, parts * planes, one, jnp.zeros((16, width), f32))
+        vec[...] = total[0:8]
+        for f in range(0, bsum.shape[0] * chunk, width):
+            bias_in[f // chunk, 0:1, f % chunk:f % chunk + width] = total[5 + f // width:6 + f // width]
+
+    def gather_sent():
+        for d in range(1, planes):
+            spread_z(d).wait_send()
+        for d in range(1, quads):
+            spread_out(d).wait_send()
+            spread_in(d).wait_send()
+        for q in range(quads):
+            pair_in(q).wait_send()
+        for origin in range(planes):
+            pair_out(origin).wait_send()
+
+            @pl.when((plane < last) & (origin <= plane))
+            def _():
+                relay(origin, 1).wait_send()
+
+            @pl.when((plane > 0) & (origin >= plane))
+            def _():
+                relay(origin, 0).wait_send()
+
+    def weight(m, c):
+        n = chunk // (2 * planes * shard)
+        at = pl.ds(c * n, n)
+        block = w0[at, :, :, 0:shard, :] if m == 0 else w1[at]
+        return block.reshape(chunk, width)
+
+    def told(sem, k):
+        pl.semaphore_wait(sem.at[lax.rem(k, slots)], parts - 1)
 
     one_way = (send1, recv1, ss1, rs1)
     way_back = (send2, recv2, ss2, rs2)
@@ -381,16 +520,15 @@
 
     def sequence_job(k, before_send):
         wait_recvs(*one_way, k)
-        radix_step(recv1.at[lax.rem(k, jobs)], tw, t_ref, parts, pairs, span)
-        o_ref[...] = dot_nn(t_ref[...], wd[...])
-        before_send()
+        radix_step(recv1.at[lax.rem(k, slots)], tw, t_ref, parts, pairs, span)
         slot = lax.rem(k, 2)
-
-        def one(u, carry):
+        half = span // 2
+
+        def one(u, base, carry):
             def put(p, rows, cols, value):
                 send2[slot, p, rows, cols] = value
 
-            spread_step(o_ref, put, me, parts, pairs, span, u)
+            spread_step(o_ref, put, me, parts, pairs, u, base)
             for h in range(2):
                 d = lax.rem(2 * u + h - me + parts, parts)
 
@@ -403,41 +541,57 @@
                     own(send2, recv2, rs2, k).start()
             return carry
 
-        lax.fori_loop(0, parts // 2, one, 0)
+        for base in range(2):
+            o_ref[...] = dot_nn(t_ref[...], wd[:, base * half:(base + 1) * half])
+            if base == 0:
+                before_send()
+            lax.fori_loop(base * parts // 4, (base + 1) * parts // 4, partial(lambda b, u, c: one(u, b, c), base), 0)
 
     def mixed_job(k):
         wait_recvs(*way_back, k)
-        blocks = recv2[lax.rem(k, jobs)].reshape(width, span)
+        blocks = recv2[lax.rem(k, slots)].reshape(width, span)
         natural = dot_tn(blocks, cp[...])
         step = span // parts
         for b in range(parts):
             for c in range(width // 128):
                 nbuf[c, pl.ds(b, step, stride=parts), :] = natural[b * step:(b + 1) * step, c * 128:(c + 1) * 128]
 
+    gather_start()
     load_of(jobs).wait()
-    for k in range(2):
-        load_of(k).wait()
-
-    def lead(k, carry):
-        hidden_job(k)
-        return carry
-
-    lax.fori_loop(0, 2, lead, 0)
+    load_of(0).wait()
+    hidden_job(0)
     dw[...] = jnp.zeros_like(dw)
     sums[...] = jnp.zeros_like(sums)
     bsum[...] = jnp.zeros_like(bsum)
-    for k in (2, 3, jobs + 1, jobs + 2):
+    gather_out()
+    gather_in()
+    for k in (1, 2, 3, jobs + 1, jobs + 2):
         load_of(k).wait()
 
     def fill(k, carry):
         sequence_job(k, lambda: None)
         tell(free1, k)
-        wait_sends(*one_way, k)
-        hidden_job(k + 2)
+
+        @pl.when(k == 0)
+        def _():
+            relay_step(0)
+            gather_pass()
+
+        @pl.when(k == 1)
+        def _():
+            wait_sends(*one_way, 0)
+
+        hidden_job(k + 1)
         return carry
 
     lax.fori_loop(0, 2, fill, 0)
-    pltpu.make_async_copy(w, w, load.at[jobs + 3]).wait()
+    relay_step(1)
+    wait_sends(*one_way, 1)
+    told(free1, 0)
+    hidden_job(3)
+    relay_step(2)
+    gather_end()
+    gather_sent()
 
     def out_copy(i):
         return pltpu.make_async_copy(outv, out.at[i], io.at[0])
@@ -452,20 +606,20 @@
         cot_copy(i).start()
         mixed_job(i)
         tell(free2, i)
-        ffn_forward(lambda at: tokv[i, at, :], nbuf, sbuf, alow, hid, slope, acc, w, vec, bias_in, chunk, rows_step)
+        ffn_forward(lambda at: tokv[i, at, :], nbuf, sbuf, alow, hid, slope, acc, weight, vec, bias_in, rows_step)
 
         def before():
             wait_sends(*way_back, i)
 
-            @pl.when(i >= 2)
+            @pl.when(i >= 1)
             def _():
-                pl.semaphore_wait(free2.at[lax.rem(i + 2, jobs)], parts - 1)
+                told(free2, i + 2)
 
         sequence_job(i + 2, before)
 
-        @pl.when(i < 2)
-        def _():
-            tell(free1, lax.rem(i + 2, jobs))
+        @pl.when(i < 3)
+        def _():
+            tell(free1, i + 2)
 
         cot_copy(i).wait()
 
@@ -480,24 +634,19 @@
             acc[at, :] = value
             tokv[i, at, :] = value.astype(bf16)
 
-        ffn_backward(nbuf, sbuf, alow, hid, slope, acc, glow, w, dw, bsum, vec, sums, chunk, rows_step, put)
+        ffn_backward(nbuf, sbuf, alow, hid, slope, acc, glow, weight, dw, bsum, vec, sums, chunk, rows_step, put)
         row_copy(i).start()
         wait_sends(*one_way, i + 2)
-        pl.semaphore_wait(free1.at[i], parts - 1)
+        told(free1, i + jobs)
         hidden_job(i + jobs)
         row_copy(i).wait()
         return carry
 
     lax.fori_loop(0, jobs, main, 0)
 
-    core, quad = lax.rem(me, 2), me // 2
     x, y = lax.rem(quad, 2), quad // 2
-    partner = (me + 1 - 2 * core, plane)
     x_peer = (me + 2 - 4 * x, plane)
     y_peer = (me + 4 - 8 * y, plane)
-    quads = parts // 2
-    group = 2 * quads * shard
-
     def rows_at(start, count=shard):
         return pl.ds(pl.multiple_of(start, shard), count)
 
@@ -507,25 +656,21 @@
     def owned(q, c, v):
         return rows_at(((2 * q + c) * planes + target(v)) * shard)
 
-    def send(src, dst, s, r, to):
-        return pltpu.make_async_remote_copy(
-            src_ref=src, dst_ref=dst, send_sem=s, recv_sem=r, device_id=to, device_id_type=MESH)
+    keep = pl.ds(0, shard)
 
     def core_copy(v):
-        at = rows_at(v * group, group)
-        return send(w.at[0, at], w.at[1, at], s_core.at[v], r_core.at[v], partner)
+        return send(w1.at[v], w0.at[v, :, :, keep], s_core.at[v], r_core.at[v], partner)
 
     def first_copy(v, m):
-        return send(w.at[0, rows_at((planes + v) * quads * shard + 2 * m * shard, 2 * shard)],
-                    w.at[0, rows_at(v * quads * shard + 2 * m * shard, 2 * shard)],
+        return send(w1.at[2 + v // 2, lax.rem(v, 2), pl.ds(2 * m, 2)], w1.at[v // 2, lax.rem(v, 2), pl.ds(2 * m, 2)],
                     s_first.at[v, m], r_first.at[v, m], (x_peer, y_peer)[m])
 
     def next_copy(v, m):
-        return send(w.at[1, rows_at((2 * v + m) * shard)], (alow, glow)[m].at[rows_at(v * shard)],
+        return send(w0.at[0, v // 2, 2 * lax.rem(v, 2) + m, keep], (alow, glow)[m].at[rows_at(v * shard)],
                     s_next.at[v, m], r_next.at[v, m], (y_peer, x_peer)[m])
 
     def z_copy(v):
-        return send(w.at[1, rows_at((2 * planes + 2 * v) * shard, 2 * shard)], rz.at[v],
+        return send(w0.at[1, v // 2, pl.ds(2 * lax.rem(v, 2), 2), keep], rz.at[v],
                     s_z.at[v], r_z.at[v], (me, target(v)))
 
     def vec_copy(k):
@@ -535,7 +680,7 @@
     def core_step(v, carry):
         for q in range(quads):
             for m in range(2):
-                w[0, rows_at(v * group + (2 * q + m) * shard)] = dw[m, owned(q, 1 - core, v)].astype(bf16)
+                w1[v, q // 2, 2 * (q % 2) + m] = dw[m, owned(q, 1 - core, v)].astype(bf16)
         core_copy(v).start()
         return carry
 
@@ -544,12 +689,11 @@
         for q in range(quads):
             for m in range(2):
                 at = owned(q, core, v)
-                dw[m, at] += w[1, rows_at(v * group + (2 * q + m) * shard)].astype(f32)
+                dw[m, at] += w0[v, q // 2, 2 * (q % 2) + m, 0:shard, :].astype(f32)
         for k in range(2):
             for m in range(2):
                 q = 2 * k + 1 - x if m == 0 else 2 * (1 - y) + k
-                at = rows_at((planes + v) * quads * shard + (2 * m + k) * shard)
-                w[0, at] = dw[m, owned(q, core, v)].astype(bf16)
+                w1[2 + v // 2, lax.rem(v, 2), 2 * m + k] = dw[m, owned(q, core, v)].astype(bf16)
         for m in range(2):
             first_copy(v, m).start()
         return carry
@@ -560,10 +704,10 @@
         for k in range(2):
             for m in range(2):
                 q = 2 * k + x if m == 0 else 2 * y + k
-                dw[m, owned(q, core, v)] += w[0, rows_at(v * quads * shard + (2 * m + k) * shard)].astype(f32)
+                dw[m, owned(q, core, v)] += w1[v // 2, lax.rem(v, 2), 2 * m + k].astype(f32)
         for m in range(2):
             q = 2 * (1 - y) + x if m == 0 else 2 * y + 1 - x
-            w[1, rows_at((2 * v + m) * shard)] = dw[m, owned(q, core, v)].astype(bf16)
+            w0[0, v // 2, 2 * lax.rem(v, 2) + m, 0:shard, :] = dw[m, owned(q, core, v)].astype(bf16)
             next_copy(v, m).start()
         return carry
 
@@ -575,8 +719,7 @@
         @pl.when(v < planes - 1)
         def _():
             for m in range(2):
-                at = rows_at((2 * planes + 2 * v + m) * shard)
-                w[1, at] = dw[m, owned(quad, core, v)].astype(bf16)
+                w0[1, v // 2, 2 * lax.rem(v, 2) + m, 0:shard, :] = dw[m, owned(quad, core, v)].astype(bf16)
             z_copy(v).start()
 
         return carry
@@ -611,9 +754,13 @@
     def drain(i, carry):
         final(i)
 
+        @pl.when(i == 0)
+        def _():
+            tell(free2, jobs)
+
         def before():
             wait_sends(*way_back, i + 4)
-            pl.semaphore_wait(free2.at[i + 2], parts - 1)
+            told(free2, i + 6)
 
         sequence_job(i + 6, before)
 
@@ -660,7 +807,7 @@
     for v in range(planes - 1):
         z_copy(v).wait_recv()
         for m in range(2):
-            dw_own[m] += rz[v, m * shard:(m + 1) * shard].astype(f32)
+            dw_own[m] += rz[v, m].astype(f32)
     total = sv[3]
     for k in range(3, 2 + planes):
         vec_copy(k).wait_recv()
@@ -683,15 +830,16 @@
         gt_copy(i).wait()
 
 
-def layer_call(tok, cot, w_all, vec, bias_in, parts, planes):
+def layer_call(tok, cot, win_own, wout_own, vec_own, parts, planes):
     jobs, span, width = tok.shape
-    ff = bias_in.size
-    shard = ff // (parts * planes)
+    shard = wout_own.shape[0]
+    ff = shard * parts * planes
     pairs = width // 2 // parts
-    chunk, rows_step = ff // 3, span // 2
+    chunk, rows_step = ff // 2, span // 2
     steps = ff // chunk
     length = span * parts
-    geo = (parts, pairs, span, width, jobs, chunk, rows_step, planes)
+    slots = 3
+    geo = (parts, pairs, span, width, jobs, slots, chunk, rows_step, planes)
     tables = (
         jnp.asarray(packed_hidden(width, parts)),
         jnp.asarray(inner_table(span, length)),
@@ -704,17 +852,18 @@
         pltpu.VMEM((jobs, span, width), bf16),
         pltpu.VMEM((span, width), bf16),
         pltpu.VMEM((span, width), bf16),
-        pltpu.VMEM((2, ff, width), bf16),
+        pltpu.VMEM((parts // 2, 2, planes, shard + 16, width), bf16),
+        pltpu.VMEM((parts // 2, 2, planes, shard, width), bf16),
         pltpu.VMEM((width, width), bf16),
         pltpu.VMEM((2 * span, span), bf16),
         pltpu.VMEM((width, width), bf16),
         pltpu.VMEM((2, ff, width), f32),
         pltpu.VMEM((2,) + block, bf16),
-        pltpu.VMEM((jobs,) + block, bf16),
+        pltpu.VMEM((slots,) + block, bf16),
         pltpu.VMEM((2,) + block, bf16),
-        pltpu.VMEM((jobs,) + block, bf16),
+        pltpu.VMEM((slots,) + block, bf16),
         pltpu.VMEM((2 * parts * pairs + 16, 2 * span), bf16),
-        pltpu.VMEM((2 * parts * pairs + 16, span), f32),
+        pltpu.VMEM((2 * parts * pairs + 16, span // 2), f32),
         pltpu.VMEM((width // 128, span, 128), f32),
         pltpu.VMEM((span, 128), f32),
         pltpu.VMEM((span, width), bf16),
@@ -724,15 +873,19 @@
         pltpu.VMEM((span, width), bf16),
         pltpu.VMEM((5, 8, width), f32),
         pltpu.VMEM((steps, 8, chunk), f32),
-        pltpu.VMEM((planes - 1, 2 * shard, width), bf16),
+        pltpu.VMEM((planes - 1, 2, shard, width), bf16),
         pltpu.VMEM((4, 16, width), f32),
         pltpu.VMEM((2 + planes, 16, width), f32),
-        dma((2, parts)), dma((jobs, parts)), dma((2, parts)), dma((jobs, parts)),
-        pltpu.SemaphoreType.REGULAR((jobs,)), pltpu.SemaphoreType.REGULAR((jobs,)),
-        dma((jobs + 4,)), dma((4 + jobs,)),
+        pltpu.VMEM((8, width), f32),
+        pltpu.VMEM((steps, 1, chunk), f32),
+        dma((2, parts)), dma((slots, parts)), dma((2, parts)), dma((slots, parts)),
+        pltpu.SemaphoreType.REGULAR((slots,)), pltpu.SemaphoreType.REGULAR((slots,)),
+        dma((jobs + 6,)), dma((4 + jobs,)),
         dma((planes,)), dma((planes,)), dma((planes, 2)), dma((planes, 2)), dma((planes, 2)), dma((planes, 2)),
         dma((planes - 1,)), dma((planes - 1,)), dma((2 + planes,)), dma((2 + planes,)),
         pltpu.SemaphoreType.REGULAR((3,)),
+        dma((3, max(parts // 2, planes))), dma((3, max(parts // 2, planes))), dma((2, planes)), dma((planes,)),
+        dma((2, max(parts // 2, planes))), dma((2, max(parts // 2, planes))),
     ]
     shape = jax.ShapeDtypeStruct
     return pl.pallas_call(
@@ -744,13 +897,13 @@
             shape((2, shard, width), f32),
             shape((16, width), f32),
         ),
-        in_specs=[hbm] * 6 + [vmem] * 3,
+        in_specs=[hbm] * 8 + [vmem],
         out_specs=(hbm,) * 3 + (vmem,) * 2,
         scratch_shapes=scratch,
         compiler_params=pltpu.CompilerParams(
             collective_id=1, has_side_effects=True, vmem_limit_bytes=64 * 1024 * 1024 - 256 * 1024),
         name="encoder_layer",
-    )(tok, cot, w_all, tables[0], tables[1], tables[2], tables[3], vec, bias_in.reshape(steps, 1, chunk))
+    )(tok, cot, win_own, wout_own, vec_own, *tables)
 
 
 def local_fast(tokens, w_in, b_in, w_out, b_out, gain_one, shift_one, gain_two, shift_two, cotangent):
@@ -759,19 +912,16 @@
     width = tokens.shape[2]
     shard = w_in.shape[1]
     planes = lax.axis_size("batch")
-    pad = 16 * width - shard - 5 * b_out.shape[0]
-    vectors = jnp.concatenate([b_in, gain_one, shift_one, gain_two, shift_two, b_out, jnp.zeros((pad,), bf16)])
-    packed = jnp.concatenate([w_in.T, w_out, vectors.reshape(16, width)], axis=0)
-    w_all = lax.all_gather(packed, both, axis=0, tiled=False)
-    vectors = w_all[:, 2 * shard].astype(f32)
-    bias_in = vectors[:, :shard].reshape(-1)
-    vec = vectors[:, shard:shard + 5 * b_out.shape[0]].reshape(vectors.shape[0], 5, -1)
-    vec = jnp.moveaxis(vec, 1, 0).reshape(5, width)
-    vec = jnp.concatenate([vec, jnp.zeros((3, width), f32)], axis=0)
-    out, gtok, _, dw, small = layer_call(tokens, cotangent, w_all, vec, bias_in, parts, planes)
     owner = lax.axis_index("seq") * planes + lax.axis_index("batch")
+    part = b_out.shape[0]
+    vectors = jnp.zeros((5, width), bf16)
+    mine = jnp.stack([gain_one, shift_one, gain_two, shift_two, b_out])
+    vectors = lax.dynamic_update_slice(vectors, mine, (0, owner * part))
+    bias = lax.dynamic_update_slice(jnp.zeros((parts * planes * shard,), bf16), b_in, (owner * shard,))
+    bias = bias.reshape(-1, width)
+    vectors = jnp.concatenate([vectors, bias, jnp.zeros((11 - bias.shape[0], width), bf16)])
+    out, gtok, _, dw, small = layer_call(tokens, cotangent, w_in.T, w_out, vectors, parts, planes)
     grad_b_in = lax.dynamic_slice(small[5:9].reshape(-1), (owner * shard,), (shard,))
-    part = b_out.shape[0]
     rest = lax.dynamic_slice(small[:5], (0, owner * part), (5, part))
     return (out, gtok, dw[0].T, grad_b_in, dw[1], rest[4], rest[0], rest[1], rest[2], rest[3])
 

time: 347 us -> 298 us (0.86)
  waiting for transfers between devices: 88.4 us -> 0 us
  Pallas kernels: 220 us -> 280 us
  between operations: 14.1 us -> 0.68 us
  local copies, waits for them, and re-layouts: 16 us -> 12.1 us
    all_gather x1 -> x0, waiting for transfers between devices: 88.4 us -> none  [local_fast(): w_all = lax.all_gather(packed, both, axis=0, tiled=False)]
    pallas_call x1, Pallas kernels: 220 us -> 280 us  [layer_call(): pl.pallas_call(partial(layer_kernel, geo), out_shape=(shape(tok.shape, bf...]
    concatenate x2 -> x1, local copies, waits for them, and re-layouts: 4.72 us -> 0.08 us  [local_fast(): jnp.concatenate([vectors, bias, jnp.zeros((11 - bias.shape[0], width), bf...]
  transfers between devices with their start and end apart: 1 -> 0, of which waited for: 1 -> 0; matrix products, arithmetic and copies ran while one was open for 0% -> 0% of each run, Pallas kernels for 0% -> 0%
where the time goes in v3:
time: 298 us; the launch traced here: 294 us
  Pallas kernels  280 us (94%)
  local copies, waits for them, and re-layouts  12.1 us (4%)
    pallas_call x1, Pallas kernels, layer_call(): pl.pallas_call(partial(layer_kernel, geo), out_shape=(shape(tok.shape, bf...  280 us

profile of v3, /device:TPU:0, one launch (start us, length us, event | category | flops | bytes accessed | tf_op | source)
XLA Modules:
  0.0 293.6 jit_solution(9477259947413667016)
XLA Ops:
  0.7 0.1 pad.2.clone
  0.7 0.7 stack.23
  1.5 0.9 dynamic_update_slice.7
  2.4 0.2 dynamic_update_slice.6
  2.5 0.7 maximum_maximum_fusion.vec_own
  3.2 280.1 %encoder_layer.1 = (bf16[4,512,768]{2,1,0:T(8,128)(2,1)}, bf16[4,512,768]{2,1,0:T(8,128)(2,1)}, f32[4,512,768]{2,1,0:T(8,128)}, f32[2,96,768]{2,1,0:T(8,128)}, f32[16,768]{1,0:T(8,128)}) custom-call(bf16[4,512,768]{2,1,0:T(8,128)(2,1)} %tok.1, bf16[4,512,768]{2,1,0:T(8,128)(2,1)} %cot.1, bf16[96,768]{1,0:T(8,128)(2,1)} %bitcast.22, ...), custom_call_target="tpu_custom_call" | custom-call | tf_op jit(solution)/shard_map/encoder_layer/pallas_call | solution.py:891
  283.3 0.8 slice.28
  284.1 0.7 slice.30
  284.9 0.1 constant_dynamic-slice_fusion
  285.0 0.5 slice_bitcast_fusion.2
  285.5 0.6 dynamic_slice.6
  286.1 1.9 slice_bitcast_fusion
  288.0 0.0 copy-start
  288.0 3.9 %copy.28 = bf16[4,512,768]{2,1,0:T(8,128)(2,1)} copy(bf16[4,512,768]{2,1,0:T(8,128)(2,1)} %get-tuple-element.35) | data formatting | bytes 6291456
  291.9 0.0 copy-done
  291.9 1.7 copy.29
  (5 shorter events, 0.0 us)
Async XLA Ops:
  288.0 3.9 %copy-start = (bf16[4,512,768]{2,1,0:T(8,128)(2,1)S(1)}, bf16[4,512,768]{2,1,0:T(8,128)(2,1)}, u32[]{:S(2)}) copy-start(bf16[4,512,768]{2,1,0:T(8,128)(2,1)} %get-tuple-element.36) | copy-start | bytes 9437188

commit v4 on v3

--- a/solution.py
+++ b/solution.py
@@ -189,7 +189,7 @@
     return value, slope
 
 
-def ffn_forward(x_get, nbuf, sbuf, alow, hid, slope, acc, weight, vec, bias_in, rows_step):
+def ffn_hidden(x_get, nbuf, sbuf, alow, hid, slope, weight, vec, bias_in, rows_step):
     rows = nbuf.shape[1]
 
     def first(r, carry):
@@ -208,22 +208,17 @@
     def step(c, carry):
         pre = dot_nt(alow[...], weight(0, c)) + bias_in[c]
         value, back = gelu_pair(pre)
-        low = value.astype(bf16)
-        hid[c] = low
+        hid[c] = value.astype(bf16)
         slope[c] = back.astype(bf16)
-        part = dot_nn(low, weight(1, c))
-
-        @pl.when(c == 0)
-        def _():
-            acc[...] = part
-
-        @pl.when(c > 0)
-        def _():
-            acc[...] += part
-
         return carry
 
     lax.fori_loop(0, hid.shape[0], step, 0)
+
+
+def ffn_branch(hid, acc, weight):
+    steps = hid.shape[0]
+    every = jnp.concatenate([hid[c] for c in range(steps)], axis=1)
+    acc[...] = dot_nn(every, weight(1, 0, steps))
 
 
 def ffn_middle(nbuf, acc, glow, cot, outv, vec, sums, rows_step):
@@ -250,17 +245,14 @@
     lax.fori_loop(0, rows // rows_step, second, 0)
 
 
-def ffn_backward(nbuf, sbuf, alow, hid, slope, acc, glow, weight, dw, bsum, vec, sums, chunk, rows_step, put):
+def ffn_backward(nbuf, sbuf, alow, hid, slope, acc, glow, weight, dw, bsum, vec, sums, chunk, rows_step, put, after):
     rows = nbuf.shape[1]
 
     def step(c, carry):
-        at = pl.ds(pl.multiple_of(c * chunk, chunk), chunk)
         gh = dot_nt(glow[...], weight(1, c))
-        pre32 = gh * slope[c].astype(f32)
-        gpre = pre32.astype(bf16)
+        gpre = (gh * slope[c].astype(f32)).astype(bf16)
+        slope[c] = gpre
         bsum[c] += fold(gpre.astype(f32))
-        dw[1, at, :] += dot_tn(hid[c], glow[...])
-        dw[0, at, :] += dot_tn(gpre, alow[...])
         acc[...] += dot_nn(gpre, weight(0, c))
         return carry
 
@@ -277,15 +269,24 @@
         return carry
 
     lax.fori_loop(0, rows // rows_step, last, 0)
+    after()
+
+    def grads(c, carry):
+        at = pl.ds(pl.multiple_of(c * chunk, chunk), chunk)
+        dw[1, at, :] += dot_tn(hid[c], glow[...])
+        dw[0, at, :] += dot_tn(slope[c], alow[...])
+        return carry
+
+    lax.fori_loop(0, hid.shape[0], grads, 0)
 
 
 def layer_kernel(geo, tok, cot, win_own, wout_own, vec_own, hp_all, wd_all, cp_all, tw,
                  out, gtok, grow, dw_own, small,
                  tokv, cotv, outv, w0, w1, hp, wd, cp, dw, send1, recv1, send2, recv2, t_ref, o_ref,
-                 nbuf, sbuf, alow, hid, slope, acc, glow, sums, bsum, rz, sv, rv, vec, bias_in,
+                 nbuf, sbuf, alow, hid, slope, acc, glow, sums, bsum, rz, rze, rzl, sv, rv, vec, bias_in,
                  ss1, rs1, ss2, rs2, free1, free2, load, io,
                  s_core, r_core, s_first, r_first, s_next, r_next, s_z, r_z, s_vec, r_vec, ready,
-                 s_spread, r_spread, s_relay, r_relay, s_pair, r_pair):
+                 s_spread, r_spread, s_relay, r_relay, s_pair, r_pair, s_early, r_early, s_late, r_late):
     parts, pairs, span, width, jobs, slots, chunk, rows_step, planes = geo
     shard = dw.shape[1] // (parts * planes)
     me = lax.axis_index("seq")
@@ -305,7 +306,11 @@
 
     core, quad = lax.rem(me, 2), me // 2
     quads = parts // 2
+    x, y = lax.rem(quad, 2), quad // 2
     partner = (me + 1 - 2 * core, plane)
+    x_peer = (me + 2 - 4 * x, plane)
+    y_peer = (me + 4 - 8 * y, plane)
+    quad_x, quad_y = quad + 1 - 2 * x, quad + 2 - 4 * y
     last = planes - 1
 
     def send(src, dst, s, r, to):
@@ -341,10 +346,6 @@
             send_sem=ss.at[lax.rem(k, 2), d], recv_sem=rs.at[lax.rem(k, slots), d],
             device_id=(p, plane), device_id_type=MESH)
 
-    def own(send, recv, rs, k):
-        return pltpu.make_async_copy(
-            send.at[lax.rem(k, 2), me], recv.at[lax.rem(k, slots), me], rs.at[lax.rem(k, slots), 0])
-
     def wait_sends(send, recv, ss, rs, k):
         def one(d, carry):
             remote(send, recv, ss, rs, k, d).wait_send()
@@ -353,8 +354,6 @@
         lax.fori_loop(1, parts, one, 0)
 
     def wait_recvs(send, recv, ss, rs, k):
-        own(send, recv, rs, k).wait()
-
         def one(d, carry):
             source = lax.rem(me + parts - d, parts)
             slot = lax.rem(k, slots)
@@ -387,9 +386,13 @@
         block = w1.at[quad, core, plane]
         return send(block, block, s_spread.at[1, d], r_spread.at[1, d], (in_plane(d), plane))
 
-    def spread_in(d):
+    def spread_in(n):
         block = w0.at[quad, core]
-        return send(block, block, s_spread.at[2, d], r_spread.at[2, d], (in_plane(d), plane))
+        return send(block, block, s_spread.at[2, n], r_spread.at[2, n], (x_peer, y_peer)[n])
+
+    def pass_in(n):
+        block = w0.at[quad_x if n == 0 else quad_y, core, pl.ds(n * planes // 2, planes // 2)]
+        return send(block, block, s_spread.at[2, 2 + n], r_spread.at[2, 2 + n], (y_peer, x_peer)[n])
 
     def relay(origin, up):
         block = w1.at[:, core, origin]
@@ -451,20 +454,30 @@
     def gather_in():
         for d in range(1, planes):
             spread_z(d).wait_recv()
-        for d in range(1, quads):
-            spread_in(d).start()
+        for n in range(2):
+            spread_in(n).start()
         pair_in(quad).start()
 
     def gather_pass():
-        for d in range(1, quads):
-            spread_in(d).wait_recv()
-            pair_in(lax.rem(quad + quads - d, quads)).start()
-
-    def gather_end():
+        for n in range(2):
+            spread_in(n).wait_recv()
+        for n in range(2):
+            pass_in(n).start()
+        pair_in(quad_x).start()
+        pair_in(quad_y).start()
+
+    def gather_diagonal():
+        for n in range(2):
+            pass_in(n).wait_recv()
+        pair_in(quads - 1 - quad).start()
+
+    def gather_end_out():
+        for origin in range(planes):
+            pair_out(origin).wait_recv()
+
+    def gather_end_in():
         for q in range(quads):
             pair_in(q).wait_recv()
-        for origin in range(planes):
-            pair_out(origin).wait_recv()
 
         def one(o, carry):
             rest = lax.rem(o, 2 * planes)
@@ -481,7 +494,9 @@
             spread_z(d).wait_send()
         for d in range(1, quads):
             spread_out(d).wait_send()
-            spread_in(d).wait_send()
+        for n in range(2):
+            spread_in(n).wait_send()
+            pass_in(n).wait_send()
         for q in range(quads):
             pair_in(q).wait_send()
         for origin in range(planes):
@@ -495,11 +510,11 @@
             def _():
                 relay(origin, 0).wait_send()
 
-    def weight(m, c):
+    def weight(m, c, count=1):
         n = chunk // (2 * planes * shard)
-        at = pl.ds(c * n, n)
+        at = pl.ds(c * n, count * n)
         block = w0[at, :, :, 0:shard, :] if m == 0 else w1[at]
-        return block.reshape(chunk, width)
+        return block.reshape(count * chunk, width)
 
     def told(sem, k):
         pl.semaphore_wait(sem.at[lax.rem(k, slots)], parts - 1)
@@ -508,9 +523,17 @@
     way_back = (send2, recv2, ss2, rs2)
 
     def hidden_job(k):
+        @pl.when(k >= 2)
+        def _():
+            wait_sends(*one_way, k - 2)
+
+        @pl.when(k >= slots)
+        def _():
+            told(free1, k)
+
         table = dot_nt(hp[...], tokv[lax.rem(k, jobs)]).astype(bf16)
         send1[lax.rem(k, 2)] = table.reshape(parts, 2 * pairs, span)
-        own(send1, recv1, rs1, k).start()
+        recv1[lax.rem(k, slots), me] = send1[lax.rem(k, 2), me]
 
         def one(d, carry):
             remote(*one_way, k, d).start()
@@ -518,9 +541,14 @@
 
         lax.fori_loop(1, parts, one, 0)
 
-    def sequence_job(k, before_send):
+    def sequence_job(k, carry):
         wait_recvs(*one_way, k)
         radix_step(recv1.at[lax.rem(k, slots)], tw, t_ref, parts, pairs, span)
+
+        @pl.when(k < 2 * jobs - slots)
+        def _():
+            tell(free1, k)
+
         slot = lax.rem(k, 2)
         half = span // 2
 
@@ -538,14 +566,23 @@
 
                 @pl.when(d == 0)
                 def _():
-                    own(send2, recv2, rs2, k).start()
+                    recv2[lax.rem(k, slots), me] = send2[slot, me]
             return carry
 
         for base in range(2):
             o_ref[...] = dot_nn(t_ref[...], wd[:, base * half:(base + 1) * half])
             if base == 0:
-                before_send()
+
+                @pl.when(k >= 2)
+                def _():
+                    wait_sends(*way_back, k - 2)
+
+                @pl.when(k >= slots)
+                def _():
+                    told(free2, k)
+
             lax.fori_loop(base * parts // 4, (base + 1) * parts // 4, partial(lambda b, u, c: one(u, b, c), base), 0)
+        return carry
 
     def mixed_job(k):
         wait_recvs(*way_back, k)
@@ -568,30 +605,15 @@
     for k in (1, 2, 3, jobs + 1, jobs + 2):
         load_of(k).wait()
 
-    def fill(k, carry):
-        sequence_job(k, lambda: None)
-        tell(free1, k)
-
-        @pl.when(k == 0)
-        def _():
-            relay_step(0)
-            gather_pass()
-
-        @pl.when(k == 1)
-        def _():
-            wait_sends(*one_way, 0)
-
-        hidden_job(k + 1)
-        return carry
-
-    lax.fori_loop(0, 2, fill, 0)
+    sequence_job(0, 0)
+    relay_step(0)
+    gather_pass()
+    hidden_job(1)
     relay_step(1)
-    wait_sends(*one_way, 1)
-    told(free1, 0)
+    hidden_job(2)
+    gather_diagonal()
     hidden_job(3)
-    relay_step(2)
-    gather_end()
-    gather_sent()
+    gather_end_in()
 
     def out_copy(i):
         return pltpu.make_async_copy(outv, out.at[i], io.at[0])
@@ -601,26 +623,24 @@
 
     def row_copy(i):
         return pltpu.make_async_copy(acc, grow.at[i], io.at[2])
+
+    def after(i):
+        row_copy(i).start()
+        hidden_job(i + jobs)
 
     def main(i, carry):
         cot_copy(i).start()
         mixed_job(i)
         tell(free2, i)
-        ffn_forward(lambda at: tokv[i, at, :], nbuf, sbuf, alow, hid, slope, acc, weight, vec, bias_in, rows_step)
-
-        def before():
-            wait_sends(*way_back, i)
-
-            @pl.when(i >= 1)
-            def _():
-                told(free2, i + 2)
-
-        sequence_job(i + 2, before)
-
-        @pl.when(i < 3)
+        ffn_hidden(lambda at: tokv[i, at, :], nbuf, sbuf, alow, hid, slope, weight, vec, bias_in, rows_step)
+        lax.fori_loop(i + 1 + i // 3, i + 2 + i // 2 + i // 3, sequence_job, 0)
+
+        @pl.when(i == 0)
         def _():
-            tell(free1, i + 2)
-
+            relay_step(2)
+            gather_end_out()
+
+        ffn_branch(hid, acc, weight)
         cot_copy(i).wait()
 
         @pl.when(i > 0)
@@ -634,19 +654,15 @@
             acc[at, :] = value
             tokv[i, at, :] = value.astype(bf16)
 
-        ffn_backward(nbuf, sbuf, alow, hid, slope, acc, glow, weight, dw, bsum, vec, sums, chunk, rows_step, put)
-        row_copy(i).start()
-        wait_sends(*one_way, i + 2)
-        told(free1, i + jobs)
-        hidden_job(i + jobs)
+        ffn_backward(nbuf, sbuf, alow, hid, slope, acc, glow, weight, dw, bsum, vec, sums, chunk, rows_step, put,
+                     lambda: after(i))
         row_copy(i).wait()
         return carry
 
     lax.fori_loop(0, jobs, main, 0)
 
-    x, y = lax.rem(quad, 2), quad // 2
-    x_peer = (me + 2 - 4 * x, plane)
-    y_peer = (me + 4 - 8 * y, plane)
+    most = shard - 16
+
     def rows_at(start, count=shard):
         return pl.ds(pl.multiple_of(start, shard), count)
 
@@ -656,22 +672,32 @@
     def owned(q, c, v):
         return rows_at(((2 * q + c) * planes + target(v)) * shard)
 
-    keep = pl.ds(0, shard)
+    keep, head, tail = pl.ds(0, shard), pl.ds(0, most), pl.ds(shard, 16)
 
     def core_copy(v):
         return send(w1.at[v], w0.at[v, :, :, keep], s_core.at[v], r_core.at[v], partner)
 
     def first_copy(v, m):
-        return send(w1.at[2 + v // 2, lax.rem(v, 2), pl.ds(2 * m, 2)], w1.at[v // 2, lax.rem(v, 2), pl.ds(2 * m, 2)],
+        at = pl.ds(2 * m, 2)
+        return send(w1.at[2 + v // 2, lax.rem(v, 2), at, head], w1.at[v // 2, lax.rem(v, 2), at, head],
                     s_first.at[v, m], r_first.at[v, m], (x_peer, y_peer)[m])
 
     def next_copy(v, m):
-        return send(w0.at[0, v // 2, 2 * lax.rem(v, 2) + m, keep], (alow, glow)[m].at[rows_at(v * shard)],
+        return send(w0.at[0, v // 2, 2 * lax.rem(v, 2) + m, head],
+                    (alow, glow)[m].at[pl.ds(pl.multiple_of(v * most, most), most)],
                     s_next.at[v, m], r_next.at[v, m], (y_peer, x_peer)[m])
 
     def z_copy(v):
-        return send(w0.at[1, v // 2, pl.ds(2 * lax.rem(v, 2), 2), keep], rz.at[v],
+        return send(w0.at[1, v // 2, pl.ds(2 * lax.rem(v, 2), 2), head], rz.at[v],
                     s_z.at[v], r_z.at[v], (me, target(v)))
+
+    def early_copy(v):
+        return send(w0.at[v, :, :, tail], rze.at[v], s_early.at[v], r_early.at[v], (me, target(v)))
+
+    def late_copy(d):
+        q = lax.rem(quad + d, quads)
+        return send(w0.at[quads - 1, q // 2, pl.ds(2 * lax.rem(q, 2), 2), tail], rzl.at[d - 1],
+                    s_late.at[d - 1], r_late.at[d - 1], (in_plane(d), plane))
 
     def vec_copy(k):
         to = (partner, x_peer, y_peer)[k] if k < 3 else (me, target(k - 3))
@@ -683,6 +709,12 @@
                 w1[v, q // 2, 2 * (q % 2) + m] = dw[m, owned(q, 1 - core, v)].astype(bf16)
         core_copy(v).start()
         return carry
+
+    def owned_most(q, v):
+        return rows_at(((2 * q + core) * planes + target(v)) * shard, most)
+
+    def owned_rest(q, v):
+        return pl.ds(pl.multiple_of(((2 * q + core) * planes + target(v)) * shard + most, 16), 16)
 
     def first_step(v, carry):
         core_copy(v).wait_recv()
@@ -690,10 +722,18 @@
             for m in range(2):
                 at = owned(q, core, v)
                 dw[m, at] += w0[v, q // 2, 2 * (q % 2) + m, 0:shard, :].astype(f32)
+
+        @pl.when(v < last)
+        def _():
+            for q in range(quads):
+                for m in range(2):
+                    w0[v, q // 2, 2 * (q % 2) + m, shard:shard + 16, :] = dw[m, owned_rest(q, v)].astype(bf16)
+            early_copy(v).start()
+
         for k in range(2):
             for m in range(2):
                 q = 2 * k + 1 - x if m == 0 else 2 * (1 - y) + k
-                w1[2 + v // 2, lax.rem(v, 2), 2 * m + k] = dw[m, owned(q, core, v)].astype(bf16)
+                w1[2 + v // 2, lax.rem(v, 2), 2 * m + k, 0:most, :] = dw[m, owned_most(q, v)].astype(bf16)
         for m in range(2):
             first_copy(v, m).start()
         return carry
@@ -704,25 +744,39 @@
         for k in range(2):
             for m in range(2):
                 q = 2 * k + x if m == 0 else 2 * y + k
-                dw[m, owned(q, core, v)] += w1[v // 2, lax.rem(v, 2), 2 * m + k].astype(f32)
+                dw[m, owned_most(q, v)] += w1[v // 2, lax.rem(v, 2), 2 * m + k, 0:most, :].astype(f32)
         for m in range(2):
             q = 2 * (1 - y) + x if m == 0 else 2 * y + 1 - x
-            w0[0, v // 2, 2 * lax.rem(v, 2) + m, 0:shard, :] = dw[m, owned(q, core, v)].astype(bf16)
+            w0[0, v // 2, 2 * lax.rem(v, 2) + m, 0:most, :] = dw[m, owned_most(q, v)].astype(bf16)
             next_copy(v, m).start()
         return carry
 
     def z_step(v, carry):
         for m in range(2):
             next_copy(v, m).wait_recv()
-            dw[m, owned(quad, core, v)] += (alow, glow)[m][rows_at(v * shard)].astype(f32)
-
-        @pl.when(v < planes - 1)
+            dw[m, owned_most(quad, v)] += (alow, glow)[m][pl.ds(pl.multiple_of(v * most, most), most)].astype(f32)
+
+        @pl.when(v < last)
         def _():
             for m in range(2):
-                w0[1, v // 2, 2 * lax.rem(v, 2) + m, 0:shard, :] = dw[m, owned(quad, core, v)].astype(bf16)
+                w0[1, v // 2, 2 * lax.rem(v, 2) + m, 0:most, :] = dw[m, owned_most(quad, v)].astype(bf16)
             z_copy(v).start()
 
         return carry
+
+    def late_step():
+        for v in range(last):
+            early_copy(v).wait_recv()
+        for q in range(quads):
+            for m in range(2):
+                at = owned_rest(q, last)
+                total = dw[m, at]
+                for v in range(last):
+                    total = total + rze[v, q // 2, 2 * (q % 2) + m].astype(f32)
+                dw[m, at] = total
+                w0[quads - 1, q // 2, 2 * (q % 2) + m, shard:shard + 16, :] = total.astype(bf16)
+        for d in range(1, quads):
+            late_copy(d).start()
 
     def vec_step(k):
         if k == 0:
@@ -742,7 +796,7 @@
     def gt_copy(i):
         return pltpu.make_async_copy(tokv.at[i], gtok.at[i], io.at[4 + i])
 
-    def final(i):
+    def final(i, carry):
         back = pltpu.make_async_copy(grow.at[i], acc, io.at[2])
         back.start()
         mixed_job(i + jobs)
@@ -750,37 +804,9 @@
         for c in range(width // 128):
             tokv[i, :, c * 128:(c + 1) * 128] = (nbuf[c] + acc[:, c * 128:(c + 1) * 128]).astype(bf16)
         gt_copy(i).start()
-
-    def drain(i, carry):
-        final(i)
-
-        @pl.when(i == 0)
-        def _():
-            tell(free2, jobs)
-
-        def before():
-            wait_sends(*way_back, i + 4)
-            told(free2, i + 6)
-
-        sequence_job(i + 6, before)
-
-        @pl.when(i == 0)
-        def _():
-            lax.fori_loop(0, planes, first_step, 0)
-
-        return carry
-
-    def finish(i, carry):
-        final(i + 2)
-        wait_sends(*way_back, i + 6)
-        wait_sends(*one_way, i + 6)
-
-        @pl.when(i == 0)
-        def _():
-            lax.fori_loop(0, planes, z_step, 0)
-
-        return carry
-
+        return carry
+
+    gather_sent()
     pl.semaphore_signal(ready.at[0], inc=1, device_id=partner, device_id_type=MESH)
     pl.semaphore_wait(ready.at[0], 1)
     lax.fori_loop(0, planes, core_step, 0)
@@ -796,18 +822,33 @@
     vec_step(1)
     pl.semaphore_wait(ready.at[1], 1)
     pl.semaphore_wait(ready.at[2], 1)
-    lax.fori_loop(0, 2, drain, 0)
+    lax.fori_loop(0, planes, first_step, 0)
+    final(0, 0)
+    tell(free2, jobs)
     vec_step(2)
-    lax.fori_loop(0, planes, next_step, 0)
+    lax.fori_loop(0, planes // 2, next_step, 0)
+    sequence_job(2 * jobs - 1, 0)
+    final(1, 0)
+    lax.fori_loop(planes // 2, planes, next_step, 0)
     vec_step(3)
-    lax.fori_loop(0, 2, finish, 0)
-    own_rows = owned(quad, core, planes - 1)
+    final(2, 0)
+    lax.fori_loop(0, planes, z_step, 0)
+    late_step()
+    final(3, 0)
+    own_most, own_rest = owned_most(quad, last), owned_rest(quad, last)
+    for v in range(last):
+        z_copy(v).wait_recv()
+    for d in range(1, quads):
+        late_copy(d).wait_recv()
     for m in range(2):
-        dw_own[m] = dw[m, own_rows]
-    for v in range(planes - 1):
-        z_copy(v).wait_recv()
-        for m in range(2):
-            dw_own[m] += rz[v, m].astype(f32)
+        total = dw[m, own_most]
+        for v in range(last):
+            total = total + rz[v, m].astype(f32)
+        dw_own[m, 0:most] = total
+        total = dw[m, own_rest]
+        for d in range(1, quads):
+            total = total + rzl[d - 1, m].astype(f32)
+        dw_own[m, most:shard] = total
     total = sv[3]
     for k in range(3, 2 + planes):
         vec_copy(k).wait_recv()
@@ -821,8 +862,14 @@
         return carry
 
     lax.fori_loop(0, planes, sent, 0)
-    for v in range(planes - 1):
+    for k in range(2 * jobs - 2, 2 * jobs):
+        wait_sends(*way_back, k)
+        wait_sends(*one_way, k)
+    for v in range(last):
         z_copy(v).wait_send()
+        early_copy(v).wait_send()
+    for d in range(1, quads):
+        late_copy(d).wait_send()
     for k in range(2 + planes):
         vec_copy(k).wait_send()
     out_copy(jobs - 1).wait()
@@ -873,7 +920,9 @@
         pltpu.VMEM((span, width), bf16),
         pltpu.VMEM((5, 8, width), f32),
         pltpu.VMEM((steps, 8, chunk), f32),
-        pltpu.VMEM((planes - 1, 2, shard, width), bf16),
+        pltpu.VMEM((planes - 1, 2, shard - 16, width), bf16),
+        pltpu.VMEM((planes - 1, 2, parts // 2, 16, width), bf16),
+        pltpu.VMEM((parts // 2 - 1, 2, 16, width), bf16),
         pltpu.VMEM((4, 16, width), f32),
         pltpu.VMEM((2 + planes, 16, width), f32),
         pltpu.VMEM((8, width), f32),
@@ -886,6 +935,7 @@
         pltpu.SemaphoreType.REGULAR((3,)),
         dma((3, max(parts // 2, planes))), dma((3, max(parts // 2, planes))), dma((2, planes)), dma((planes,)),
         dma((2, max(parts // 2, planes))), dma((2, max(parts // 2, planes))),
+        dma((planes - 1,)), dma((planes - 1,)), dma((parts // 2 - 1,)), dma((parts // 2 - 1,)),
     ]
     shape = jax.ShapeDtypeStruct
     return pl.pallas_call(

time: 298 us -> 264 us (0.89); the launches traced: 294 us -> 263 us
  Pallas kernels: 280 us -> 250 us
    pallas_call x1, Pallas kernels: 280 us -> 250 us  [layer_call(): pl.pallas_call(partial(layer_kernel, geo), out_shape=(shape(tok.shape, bf...]
where the time goes in v4:
time: 264 us; the launch traced here: 263 us
  Pallas kernels  250 us (95%)
  local copies, waits for them, and re-layouts  12.1 us (5%)
    pallas_call x1, Pallas kernels, layer_call(): pl.pallas_call(partial(layer_kernel, geo), out_shape=(shape(tok.shape, bf...  250 us
    unnamed x4, local copies, waits for them, and re-layouts  5.57 us

profile of v4, /device:TPU:0, one launch (start us, length us, event | category | flops | bytes accessed | tf_op | source)
XLA Modules:
  0.0 263.1 jit_solution(4240333025875618519)
XLA Ops:
  0.7 0.1 pad.2.clone
  0.7 0.7 stack.23
  1.5 0.9 dynamic_update_slice.7
  2.4 0.2 dynamic_update_slice.6
  2.5 0.7 maximum_maximum_fusion.vec_own
  3.2 249.7 %encoder_layer.1 = (bf16[4,512,768]{2,1,0:T(8,128)(2,1)}, bf16[4,512,768]{2,1,0:T(8,128)(2,1)}, f32[4,512,768]{2,1,0:T(8,128)}, f32[2,96,768]{2,1,0:T(8,128)}, f32[16,768]{1,0:T(8,128)}) custom-call(bf16[4,512,768]{2,1,0:T(8,128)(2,1)} %tok.1, bf16[4,512,768]{2,1,0:T(8,128)(2,1)} %cot.1, bf16[96,768]{1,0:T(8,128)(2,1)} %bitcast.22, ...), custom_call_target="tpu_custom_call" | custom-call | tf_op jit(solution)/shard_map/encoder_layer/pallas_call | solution.py:941
  252.9 0.8 slice.28
  253.7 0.7 slice.30
  254.5 0.1 constant_dynamic-slice_fusion
  254.5 0.5 slice_bitcast_fusion.2
  255.1 0.6 dynamic_slice.6
  255.7 1.9 slice_bitcast_fusion
  257.6 0.0 copy-start
  257.6 3.9 %copy.28 = bf16[4,512,768]{2,1,0:T(8,128)(2,1)} copy(bf16[4,512,768]{2,1,0:T(8,128)(2,1)} %get-tuple-element.35) | data formatting | bytes 6291456
  261.5 0.0 copy-done
  261.5 1.7 copy.29
  (5 shorter events, 0.0 us)
Async XLA Ops:
  257.6 3.9 %copy-start = (bf16[4,512,768]{2,1,0:T(8,128)(2,1)S(1)}, bf16[4,512,768]{2,1,0:T(8,128)(2,1)}, u32[]{:S(2)}) copy-start(bf16[4,512,768]{2,1,0:T(8,128)(2,1)} %get-tuple-element.36) | copy-start | bytes 9437188

commit v5 on v4

--- a/solution.py
+++ b/solution.py
@@ -98,11 +98,11 @@
     groups = pairs // 16
     count = 2 * parts * pairs
 
-    def tile(u, carry):
-        lanes = pl.ds(pl.multiple_of(u * 128, 128), 128)
-        lanes_im = pl.ds(pl.multiple_of(span + u * 128, 128), 128)
+    row = lax.broadcasted_iota(jnp.int32, (16, 128), 0)
+    for u in range(span // 128):
+        lanes = pl.ds(u * 128, 128)
+        lanes_im = pl.ds(span + u * 128, 128)
         extra = [jnp.zeros((16, 128), f32), jnp.zeros((16, 128), f32)]
-        row = lax.broadcasted_iota(jnp.int32, (16, 128), 0)
         for g in range(groups):
             x = []
             for s in range(parts):
@@ -125,14 +125,11 @@
                         extra[1] = jnp.where(hit, jnp.broadcast_to(tr[0:1], (16, 128)), extra[1])
         t_ref[count:count + 16, lanes] = extra[0].astype(bf16)
         t_ref[count:count + 16, lanes_im] = extra[1].astype(bf16)
-        return carry
-
-    lax.fori_loop(0, span // 128, tile, 0)
 
 
 def spread_step(o_ref, put, me, parts, pairs, u, half):
     count = 2 * parts * pairs
-    lanes = pl.ds(pl.multiple_of((u - half * parts // 4) * 128, 128), 128)
+    lanes = pl.ds((u - half * parts // 4) * 128, 128)
     low = lax.broadcasted_iota(jnp.int32, (16, 128), 1) < 64
     row = lax.broadcasted_iota(jnp.int32, (16, 128), 0)
     special = (row == 0) & (jnp.zeros((16, 128), jnp.int32) + me == 0)
@@ -190,10 +187,8 @@
 
 
 def ffn_hidden(x_get, nbuf, sbuf, alow, hid, slope, weight, vec, bias_in, rows_step):
-    rows = nbuf.shape[1]
-
-    def first(r, carry):
-        at = pl.ds(pl.multiple_of(r * rows_step, rows_step), rows_step)
+    for r in range(0, nbuf.shape[1], rows_step):
+        at = pl.ds(r, rows_step)
         v = x_get(at).astype(f32) + rows_of(nbuf, at)
         center = v - mean_of(v)
         inv = lax.rsqrt(mean_of(center * center) + epsilon)
@@ -201,18 +196,10 @@
         set_rows(nbuf, at, n)
         sbuf[at, :] = jnp.broadcast_to(inv, (rows_step, 128))
         alow[at, :] = (n * vec[0:1] + vec[1:2]).astype(bf16)
-        return carry
-
-    lax.fori_loop(0, rows // rows_step, first, 0)
-
-    def step(c, carry):
-        pre = dot_nt(alow[...], weight(0, c)) + bias_in[c]
-        value, back = gelu_pair(pre)
+    for c in range(hid.shape[0]):
+        value, back = gelu_pair(dot_nt(alow[...], weight(0, c)) + bias_in[c])
         hid[c] = value.astype(bf16)
         slope[c] = back.astype(bf16)
-        return carry
-
-    lax.fori_loop(0, hid.shape[0], step, 0)
 
 
 def ffn_branch(hid, acc, weight):
@@ -222,10 +209,8 @@
 
 
 def ffn_middle(nbuf, acc, glow, cot, outv, vec, sums, rows_step):
-    rows = nbuf.shape[1]
-
-    def second(r, carry):
-        at = pl.ds(pl.multiple_of(r * rows_step, rows_step), rows_step)
+    for r in range(0, nbuf.shape[1], rows_step):
+        at = pl.ds(r, rows_step)
         v = rows_of(nbuf, at) * vec[0:1] + vec[1:2] + (acc[at, :] + vec[4:5])
         center = v - mean_of(v)
         inv = lax.rsqrt(mean_of(center * center) + epsilon)
@@ -240,44 +225,31 @@
         sums[2] += fold(g * n)
         sums[3] += fold(g)
         sums[4] += fold(low.astype(f32))
-        return carry
-
-    lax.fori_loop(0, rows // rows_step, second, 0)
-
-
-def ffn_backward(nbuf, sbuf, alow, hid, slope, acc, glow, weight, dw, bsum, vec, sums, chunk, rows_step, put, after):
-    rows = nbuf.shape[1]
-
-    def step(c, carry):
+
+
+def ffn_backward(nbuf, sbuf, hid, slope, acc, glow, weight, bsum, vec, sums, rows_step, put):
+    for c in range(hid.shape[0]):
         gh = dot_nt(glow[...], weight(1, c))
         gpre = (gh * slope[c].astype(f32)).astype(bf16)
         slope[c] = gpre
         bsum[c] += fold(gpre.astype(f32))
         acc[...] += dot_nn(gpre, weight(0, c))
-        return carry
-
-    lax.fori_loop(0, hid.shape[0], step, 0)
-
-    def last(r, carry):
-        at = pl.ds(pl.multiple_of(r * rows_step, rows_step), rows_step)
+    for r in range(0, nbuf.shape[1], rows_step):
+        at = pl.ds(r, rows_step)
         ga = acc[at, :]
         n = rows_of(nbuf, at)
         sums[0] += fold(ga * n)
         sums[1] += fold(ga)
         q = ga * vec[0:1]
         put(at, sbuf[at, 0:1] * (q - mean_of(q) - n * mean_of(q * n)))
-        return carry
-
-    lax.fori_loop(0, rows // rows_step, last, 0)
-    after()
-
-    def grads(c, carry):
-        at = pl.ds(pl.multiple_of(c * chunk, chunk), chunk)
+
+
+def ffn_grads(alow, hid, slope, glow, dw):
+    chunk = hid.shape[2]
+    for c in range(hid.shape[0]):
+        at = pl.ds(c * chunk, chunk)
         dw[1, at, :] += dot_tn(hid[c], glow[...])
         dw[0, at, :] += dot_tn(slope[c], alow[...])
-        return carry
-
-    lax.fori_loop(0, hid.shape[0], grads, 0)
 
 
 def layer_kernel(geo, tok, cot, win_own, wout_own, vec_own, hp_all, wd_all, cp_all, tw,
@@ -549,39 +521,31 @@
         def _():
             tell(free1, k)
 
+        @pl.when(k >= 2)
+        def _():
+            wait_sends(*way_back, k - 2)
+
+        @pl.when(k >= slots)
+        def _():
+            told(free2, k)
+
         slot = lax.rem(k, 2)
         half = span // 2
 
-        def one(u, base, carry):
-            def put(p, rows, cols, value):
-                send2[slot, p, rows, cols] = value
-
-            spread_step(o_ref, put, me, parts, pairs, u, base)
-            for h in range(2):
-                d = lax.rem(2 * u + h - me + parts, parts)
-
-                @pl.when(d > 0)
-                def _():
-                    remote(*way_back, k, d).start()
-
-                @pl.when(d == 0)
-                def _():
-                    recv2[lax.rem(k, slots), me] = send2[slot, me]
-            return carry
+        def put(p, rows, cols, value):
+            send2[slot, p, rows, cols] = value
 
         for base in range(2):
             o_ref[...] = dot_nn(t_ref[...], wd[:, base * half:(base + 1) * half])
-            if base == 0:
-
-                @pl.when(k >= 2)
-                def _():
-                    wait_sends(*way_back, k - 2)
-
-                @pl.when(k >= slots)
-                def _():
-                    told(free2, k)
-
-            lax.fori_loop(base * parts // 4, (base + 1) * parts // 4, partial(lambda b, u, c: one(u, b, c), base), 0)
+            for u in range(base * parts // 4, (base + 1) * parts // 4):
+                spread_step(o_ref, put, me, parts, pairs, u, base)
+        recv2[lax.rem(k, slots), me] = send2[slot, me]
+
+        def one(d, carry):
+            remote(*way_back, k, d).start()
+            return carry
+
+        lax.fori_loop(1, parts, one, 0)
         return carry
 
     def mixed_job(k):
@@ -624,10 +588,6 @@
     def row_copy(i):
         return pltpu.make_async_copy(acc, grow.at[i], io.at[2])
 
-    def after(i):
-        row_copy(i).start()
-        hidden_job(i + jobs)
-
     def main(i, carry):
         cot_copy(i).start()
         mixed_job(i)
@@ -654,8 +614,10 @@
             acc[at, :] = value
             tokv[i, at, :] = value.astype(bf16)
 
-        ffn_backward(nbuf, sbuf, alow, hid, slope, acc, glow, weight, dw, bsum, vec, sums, chunk, rows_step, put,
-                     lambda: after(i))
+        ffn_backward(nbuf, sbuf, hid, slope, acc, glow, weight, bsum, vec, sums, rows_step, put)
+        row_copy(i).start()
+        hidden_job(i + jobs)
+        ffn_grads(alow, hid, slope, glow, dw)
         row_copy(i).wait()
         return carry
 
@@ -882,7 +844,7 @@
     shard = wout_own.shape[0]
     ff = shard * parts * planes
     pairs = width // 2 // parts
-    chunk, rows_step = ff // 2, span // 2
+    chunk, rows_step = ff // (parts // 2), span // 4
     steps = ff // chunk
     length = span * parts
     slots = 3

time: 264 us -> 255 us (0.966)
  Pallas kernels: 250 us -> 241 us
    pallas_call x1, Pallas kernels: 250 us -> 241 us  [layer_call(): pl.pallas_call(partial(layer_kernel, geo), out_shape=(shape(tok.shape, bf...]
where the time goes in v5:
time: 255 us; the launch traced here: 254 us
  Pallas kernels  241 us (95%)
  local copies, waits for them, and re-layouts  12.1 us (5%)
    pallas_call x1, Pallas kernels, layer_call(): pl.pallas_call(partial(layer_kernel, geo), out_shape=(shape(tok.shape, bf...  241 us
    unnamed x4, local copies, waits for them, and re-layouts  5.57 us

profile of v5, /device:TPU:0, one launch (start us, length us, event | category | flops | bytes accessed | tf_op | source)
XLA Modules:
  0.0 254.2 jit_solution(4572748751040653957)
XLA Ops:
  0.7 0.1 pad.2.clone
  0.7 0.7 stack.23
  1.5 0.9 dynamic_update_slice.7
  2.4 0.2 dynamic_update_slice.6
  2.5 0.7 maximum_maximum_fusion.vec_own
  3.2 240.8 %encoder_layer.1 = (bf16[4,512,768]{2,1,0:T(8,128)(2,1)}, bf16[4,512,768]{2,1,0:T(8,128)(2,1)}, f32[4,512,768]{2,1,0:T(8,128)}, f32[2,96,768]{2,1,0:T(8,128)}, f32[16,768]{1,0:T(8,128)}) custom-call(bf16[4,512,768]{2,1,0:T(8,128)(2,1)} %tok.1, bf16[4,512,768]{2,1,0:T(8,128)(2,1)} %cot.1, bf16[96,768]{1,0:T(8,128)(2,1)} %bitcast.22, ...), custom_call_target="tpu_custom_call" | custom-call | tf_op jit(solution)/shard_map/encoder_layer/pallas_call | solution.py:903
  244.0 0.8 slice.28
  244.8 0.7 slice.30
  245.5 0.1 constant_dynamic-slice_fusion
  245.6 0.5 slice_bitcast_fusion.2
  246.1 0.6 dynamic_slice.6
  246.7 1.9 slice_bitcast_fusion
  248.6 0.0 copy-start
  248.6 3.9 %copy.28 = bf16[4,512,768]{2,1,0:T(8,128)(2,1)} copy(bf16[4,512,768]{2,1,0:T(8,128)(2,1)} %get-tuple-element.35) | data formatting | bytes 6291456
  252.5 0.0 copy-done
  252.5 1.7 copy.29
  (5 shorter events, 0.0 us)
Async XLA Ops:
  248.6 3.9 %copy-start = (bf16[4,512,768]{2,1,0:T(8,128)(2,1)S(1)}, bf16[4,512,768]{2,1,0:T(8,128)(2,1)}, u32[]{:S(2)}) copy-start(bf16[4,512,768]{2,1,0:T(8,128)(2,1)} %get-tuple-element.36) | copy-start | bytes 9437188

commit v6 on v5

--- a/solution.py
+++ b/solution.py
@@ -252,13 +252,14 @@
         dw[0, at, :] += dot_tn(slope[c], alow[...])
 
 
-def layer_kernel(geo, tok, cot, win_own, wout_own, vec_own, hp_all, wd_all, cp_all, tw,
-                 out, gtok, grow, dw_own, small,
+def layer_kernel(geo, tok, cot, win_own, wout_own, hp_all, wd_all, cp_all, tw, b_in, *rest):
+    vec_own = rest[:5]
+    (out, gtok, grow, dwin_own, dwout_own, small,
                  tokv, cotv, outv, w0, w1, hp, wd, cp, dw, send1, recv1, send2, recv2, t_ref, o_ref,
-                 nbuf, sbuf, alow, hid, slope, acc, glow, sums, bsum, rz, rze, rzl, sv, rv, vec, bias_in,
+                 nbuf, sbuf, alow, hid, slope, acc, glow, sums, bsum, rz, rze, rzl, sv, rv, va, ra, vec, bias_in,
                  ss1, rs1, ss2, rs2, free1, free2, load, io,
                  s_core, r_core, s_first, r_first, s_next, r_next, s_z, r_z, s_vec, r_vec, ready,
-                 s_spread, r_spread, s_relay, r_relay, s_pair, r_pair, s_early, r_early, s_late, r_late):
+                 s_spread, r_spread, s_relay, r_relay, s_pair, r_pair, s_early, r_early, s_late, r_late, s_va, r_va) = rest[5:]
     parts, pairs, span, width, jobs, slots, chunk, rows_step, planes = geo
     shard = dw.shape[1] // (parts * planes)
     me = lax.axis_index("seq")
@@ -290,12 +291,27 @@
             src_ref=src, dst_ref=dst, send_sem=s, recv_sem=r, device_id=to, device_id_type=MESH)
 
     own_loads = (
-        pltpu.make_async_copy(win_own, w0.at[quad, core, plane, pl.ds(0, shard)], load.at[jobs + 3]),
-        pltpu.make_async_copy(vec_own, w0.at[quad, core, plane, pl.ds(shard, 16)], load.at[jobs + 4]),
-        pltpu.make_async_copy(wout_own, w1.at[quad, core, plane], load.at[jobs + 5]),
+        pltpu.make_async_copy(win_own, w0.at[quad, core, plane], load.at[jobs + 3]),
+        pltpu.make_async_copy(wout_own, w1.at[quad, core, plane], load.at[jobs + 4]),
     )
     for copy in own_loads:
         copy.start()
+
+    owner = me * planes + plane
+    part = width // (parts * planes)
+    per_row = width // shard
+    bias_row = 5 + owner // per_row
+    row16 = lax.broadcasted_iota(jnp.int32, (16, width), 0)
+    is_bias = row16 == jnp.zeros((16, width), jnp.int32) + bias_row
+    sv[0] = jnp.zeros_like(sv[0])
+    for j in range(5):
+        sv[0, j:j + 1, 0:part] = vec_own[j][...].astype(f32)
+    sv[0, 8:9, 0:shard] = b_in[...].astype(f32)
+    rows8 = pltpu.roll(sv[0, 0:8], owner * part, 1)
+    bias8 = pltpu.roll(sv[0, 8:16], lax.rem(owner, per_row) * shard, 1)
+    placed = jnp.concatenate([rows8, jnp.zeros((8, width), f32)], axis=0)
+    placed = jnp.where(is_bias, jnp.broadcast_to(bias8[0:1], (16, width)), placed)
+    va[0] = placed.astype(bf16)
 
     barrier = pltpu.get_barrier_semaphore()
 
@@ -363,7 +379,7 @@
         return send(block, block, s_spread.at[2, n], r_spread.at[2, n], (x_peer, y_peer)[n])
 
     def pass_in(n):
-        block = w0.at[quad_x if n == 0 else quad_y, core, pl.ds(n * planes // 2, planes // 2)]
+        block = w0.at[(quad_x, quad_y)[n], core, pl.ds(n * planes // 2, planes // 2)]
         return send(block, block, s_spread.at[2, 2 + n], r_spread.at[2, 2 + n], (y_peer, x_peer)[n])
 
     def relay(origin, up):
@@ -400,6 +416,17 @@
                 relay(above, 0).start()
 
             pair_out(above).start()
+
+    def vec_spread(k):
+        to = (partner, x_peer, y_peer)[k] if k < 3 else (me, along(k - 2))
+        return send(va.at[min(k, 3)], ra.at[k], s_va.at[k], r_va.at[k], to)
+
+    def vec_gather(k):
+        if k > 0:
+            vec_spread(k - 1).wait_recv()
+            va[k] = (va[k - 1].astype(f32) + ra[k - 1].astype(f32)).astype(bf16)
+        for j in ((k,) if k < 3 else range(3, 2 + planes)):
+            vec_spread(j).start()
 
     def gather_start():
         for copy in own_loads:
@@ -451,17 +478,17 @@
         for q in range(quads):
             pair_in(q).wait_recv()
 
-        def one(o, carry):
-            rest = lax.rem(o, 2 * planes)
-            block = w0[o // (2 * planes), rest // planes, lax.rem(rest, planes), shard:shard + 16, :]
-            return carry + block.astype(f32)
-
-        total = lax.fori_loop(0, parts * planes, one, jnp.zeros((16, width), f32))
+        total = va[3].astype(f32)
+        for k in range(3, 2 + planes):
+            vec_spread(k).wait_recv()
+            total = total + ra[k].astype(f32)
         vec[...] = total[0:8]
         for f in range(0, bsum.shape[0] * chunk, width):
             bias_in[f // chunk, 0:1, f % chunk:f % chunk + width] = total[5 + f // width:6 + f // width]
 
     def gather_sent():
+        for k in range(2 + planes):
+            vec_spread(k).wait_send()
         for d in range(1, planes):
             spread_z(d).wait_send()
         for d in range(1, quads):
@@ -485,7 +512,7 @@
     def weight(m, c, count=1):
         n = chunk // (2 * planes * shard)
         at = pl.ds(c * n, count * n)
-        block = w0[at, :, :, 0:shard, :] if m == 0 else w1[at]
+        block = w0[at] if m == 0 else w1[at]
         return block.reshape(count * chunk, width)
 
     def told(sem, k):
@@ -557,7 +584,9 @@
             for c in range(width // 128):
                 nbuf[c, pl.ds(b, step, stride=parts), :] = natural[b * step:(b + 1) * step, c * 128:(c + 1) * 128]
 
+    vec_gather(0)
     gather_start()
+    vec_gather(1)
     load_of(jobs).wait()
     load_of(0).wait()
     hidden_job(0)
@@ -565,11 +594,13 @@
     sums[...] = jnp.zeros_like(sums)
     bsum[...] = jnp.zeros_like(bsum)
     gather_out()
+    vec_gather(2)
     gather_in()
     for k in (1, 2, 3, jobs + 1, jobs + 2):
         load_of(k).wait()
 
     sequence_job(0, 0)
+    vec_gather(3)
     relay_step(0)
     gather_pass()
     hidden_job(1)
@@ -623,7 +654,8 @@
 
     lax.fori_loop(0, jobs, main, 0)
 
-    most = shard - 16
+    rest_rows = 16
+    most = shard - rest_rows
 
     def rows_at(start, count=shard):
         return pl.ds(pl.multiple_of(start, shard), count)
@@ -634,10 +666,10 @@
     def owned(q, c, v):
         return rows_at(((2 * q + c) * planes + target(v)) * shard)
 
-    keep, head, tail = pl.ds(0, shard), pl.ds(0, most), pl.ds(shard, 16)
+    head = pl.ds(0, most)
 
     def core_copy(v):
-        return send(w1.at[v], w0.at[v, :, :, keep], s_core.at[v], r_core.at[v], partner)
+        return send(w1.at[v], w0.at[v], s_core.at[v], r_core.at[v], partner)
 
     def first_copy(v, m):
         at = pl.ds(2 * m, 2)
@@ -654,11 +686,11 @@
                     s_z.at[v], r_z.at[v], (me, target(v)))
 
     def early_copy(v):
-        return send(w0.at[v, :, :, tail], rze.at[v], s_early.at[v], r_early.at[v], (me, target(v)))
+        return send(hid.at[v, pl.ds(0, 2 * quads * rest_rows)], rze.at[v], s_early.at[v], r_early.at[v], (me, target(v)))
 
     def late_copy(d):
         q = lax.rem(quad + d, quads)
-        return send(w0.at[quads - 1, q // 2, pl.ds(2 * lax.rem(q, 2), 2), tail], rzl.at[d - 1],
+        return send(hid.at[last, pl.ds(pl.multiple_of(2 * q * rest_rows, 2 * rest_rows), 2 * rest_rows)], rzl.at[d - 1],
                     s_late.at[d - 1], r_late.at[d - 1], (in_plane(d), plane))
 
     def vec_copy(k):
@@ -676,20 +708,21 @@
         return rows_at(((2 * q + core) * planes + target(v)) * shard, most)
 
     def owned_rest(q, v):
-        return pl.ds(pl.multiple_of(((2 * q + core) * planes + target(v)) * shard + most, 16), 16)
+        return pl.ds(pl.multiple_of(((2 * q + core) * planes + target(v)) * shard + most, 16), rest_rows)
 
     def first_step(v, carry):
         core_copy(v).wait_recv()
         for q in range(quads):
             for m in range(2):
                 at = owned(q, core, v)
-                dw[m, at] += w0[v, q // 2, 2 * (q % 2) + m, 0:shard, :].astype(f32)
+                dw[m, at] += w0[v, q // 2, 2 * (q % 2) + m].astype(f32)
 
         @pl.when(v < last)
         def _():
             for q in range(quads):
                 for m in range(2):
-                    w0[v, q // 2, 2 * (q % 2) + m, shard:shard + 16, :] = dw[m, owned_rest(q, v)].astype(bf16)
+                    at = pl.ds((2 * q + m) * rest_rows, rest_rows)
+                    hid[v, at, :] = dw[m, owned_rest(q, v)].astype(bf16)
             early_copy(v).start()
 
         for k in range(2):
@@ -734,9 +767,9 @@
                 at = owned_rest(q, last)
                 total = dw[m, at]
                 for v in range(last):
-                    total = total + rze[v, q // 2, 2 * (q % 2) + m].astype(f32)
+                    total = total + rze[v, (2 * q + m) * rest_rows:(2 * q + m + 1) * rest_rows].astype(f32)
                 dw[m, at] = total
-                w0[quads - 1, q // 2, 2 * (q % 2) + m, shard:shard + 16, :] = total.astype(bf16)
+                hid[last, (2 * q + m) * rest_rows:(2 * q + m + 1) * rest_rows, :] = total.astype(bf16)
         for d in range(1, quads):
             late_copy(d).start()
 
@@ -806,16 +839,20 @@
         total = dw[m, own_most]
         for v in range(last):
             total = total + rz[v, m].astype(f32)
-        dw_own[m, 0:most] = total
+        (dwin_own, dwout_own)[m][0:most] = total
         total = dw[m, own_rest]
         for d in range(1, quads):
-            total = total + rzl[d - 1, m].astype(f32)
-        dw_own[m, most:shard] = total
+            total = total + rzl[d - 1, m * rest_rows:(m + 1) * rest_rows].astype(f32)
+        (dwin_own, dwout_own)[m][most:shard] = total
     total = sv[3]
     for k in range(3, 2 + planes):
         vec_copy(k).wait_recv()
         total = total + rv[k]
-    small[...] = total
+    mine = jnp.sum(jnp.where(is_bias, total, 0.0), axis=0, keepdims=True)
+    mine = pltpu.roll(jnp.broadcast_to(mine, (8, width)), width - lax.rem(owner, per_row) * shard, 1)
+    rows8 = pltpu.roll(total[0:8], width - owner * part, 1)
+    row8 = lax.broadcasted_iota(jnp.int32, (8, 128), 0)
+    small[...] = jnp.where(row8 == 5, mine[:, 0:128], rows8[:, 0:128])
 
     def sent(v, carry):
         for m in range(2):
@@ -839,7 +876,7 @@
         gt_copy(i).wait()
 
 
-def layer_call(tok, cot, win_own, wout_own, vec_own, parts, planes):
+def layer_call(tok, cot, win_own, wout_own, b_in, vectors, parts, planes):
     jobs, span, width = tok.shape
     shard = wout_own.shape[0]
     ff = shard * parts * planes
@@ -861,7 +898,7 @@
         pltpu.VMEM((jobs, span, width), bf16),
         pltpu.VMEM((span, width), bf16),
         pltpu.VMEM((span, width), bf16),
-        pltpu.VMEM((parts // 2, 2, planes, shard + 16, width), bf16),
+        pltpu.VMEM((parts // 2, 2, planes, shard, width), bf16),
         pltpu.VMEM((parts // 2, 2, planes, shard, width), bf16),
         pltpu.VMEM((width, width), bf16),
         pltpu.VMEM((2 * span, span), bf16),
@@ -883,21 +920,24 @@
         pltpu.VMEM((5, 8, width), f32),
         pltpu.VMEM((steps, 8, chunk), f32),
         pltpu.VMEM((planes - 1, 2, shard - 16, width), bf16),
-        pltpu.VMEM((planes - 1, 2, parts // 2, 16, width), bf16),
-        pltpu.VMEM((parts // 2 - 1, 2, 16, width), bf16),
+        pltpu.VMEM((planes - 1, parts * 16, width), bf16),
+        pltpu.VMEM((parts // 2 - 1, 2 * 16, width), bf16),
         pltpu.VMEM((4, 16, width), f32),
         pltpu.VMEM((2 + planes, 16, width), f32),
+        pltpu.VMEM((4, 16, width), bf16),
+        pltpu.VMEM((2 + planes, 16, width), bf16),
         pltpu.VMEM((8, width), f32),
         pltpu.VMEM((steps, 1, chunk), f32),
         dma((2, parts)), dma((slots, parts)), dma((2, parts)), dma((slots, parts)),
         pltpu.SemaphoreType.REGULAR((slots,)), pltpu.SemaphoreType.REGULAR((slots,)),
-        dma((jobs + 6,)), dma((4 + jobs,)),
+        dma((jobs + 5,)), dma((4 + jobs,)),
         dma((planes,)), dma((planes,)), dma((planes, 2)), dma((planes, 2)), dma((planes, 2)), dma((planes, 2)),
         dma((planes - 1,)), dma((planes - 1,)), dma((2 + planes,)), dma((2 + planes,)),
         pltpu.SemaphoreType.REGULAR((3,)),
         dma((3, max(parts // 2, planes))), dma((3, max(parts // 2, planes))), dma((2, planes)), dma((planes,)),
         dma((2, max(parts // 2, planes))), dma((2, max(parts // 2, planes))),
         dma((planes - 1,)), dma((planes - 1,)), dma((parts // 2 - 1,)), dma((parts // 2 - 1,)),
+        dma((2 + planes,)), dma((2 + planes,)),
     ]
     shape = jax.ShapeDtypeStruct
     return pl.pallas_call(
@@ -906,16 +946,17 @@
             shape(tok.shape, bf16),
             shape(tok.shape, bf16),
             shape(tok.shape, f32),
-            shape((2, shard, width), f32),
-            shape((16, width), f32),
+            shape((shard, width), f32),
+            shape((shard, width), f32),
+            shape((8, 128), f32),
         ),
-        in_specs=[hbm] * 8 + [vmem],
-        out_specs=(hbm,) * 3 + (vmem,) * 2,
+        in_specs=[hbm] * 7 + [vmem] * 7,
+        out_specs=(hbm,) * 3 + (vmem,) * 3,
         scratch_shapes=scratch,
         compiler_params=pltpu.CompilerParams(
             collective_id=1, has_side_effects=True, vmem_limit_bytes=64 * 1024 * 1024 - 256 * 1024),
         name="encoder_layer",
-    )(tok, cot, win_own, wout_own, vec_own, *tables)
+    )(tok, cot, win_own, wout_own, *tables, b_in, *vectors)
 
 
 def local_fast(tokens, w_in, b_in, w_out, b_out, gain_one, shift_one, gain_two, shift_two, cotangent):
@@ -924,18 +965,12 @@
     width = tokens.shape[2]
     shard = w_in.shape[1]
     planes = lax.axis_size("batch")
-    owner = lax.axis_index("seq") * planes + lax.axis_index("batch")
     part = b_out.shape[0]
-    vectors = jnp.zeros((5, width), bf16)
-    mine = jnp.stack([gain_one, shift_one, gain_two, shift_two, b_out])
-    vectors = lax.dynamic_update_slice(vectors, mine, (0, owner * part))
-    bias = lax.dynamic_update_slice(jnp.zeros((parts * planes * shard,), bf16), b_in, (owner * shard,))
-    bias = bias.reshape(-1, width)
-    vectors = jnp.concatenate([vectors, bias, jnp.zeros((11 - bias.shape[0], width), bf16)])
-    out, gtok, _, dw, small = layer_call(tokens, cotangent, w_in.T, w_out, vectors, parts, planes)
-    grad_b_in = lax.dynamic_slice(small[5:9].reshape(-1), (owner * shard,), (shard,))
-    rest = lax.dynamic_slice(small[:5], (0, owner * part), (5, part))
-    return (out, gtok, dw[0].T, grad_b_in, dw[1], rest[4], rest[0], rest[1], rest[2], rest[3])
+    vectors = [v.reshape(1, part) for v in (gain_one, shift_one, gain_two, shift_two, b_out)]
+    out, gtok, _, dwin, dwout, small = layer_call(
+        tokens, cotangent, w_in.T, w_out, b_in.reshape(1, shard), vectors, parts, planes)
+    rest = small[:5, :part]
+    return (out, gtok, dwin.T, small[5, :shard], dwout, rest[4], rest[0], rest[1], rest[2], rest[3])
 
 
 def hidden_table(extent):

time: 255 us -> 245 us (0.961)
  Pallas kernels: 241 us -> 235 us
    pallas_call x1, Pallas kernels: 241 us -> 235 us  [layer_call(): pl.pallas_call(partial(layer_kernel, geo), out_shape=(shape(tok.shape, bf...]
    unnamed x4 -> x10, local copies, waits for them, and re-layouts: 5.57 us -> 7.01 us
where the time goes in v6:
time: 245 us
  Pallas kernels  235 us (96%)
  local copies, waits for them, and re-layouts  9.58 us (4%)
    pallas_call x1, Pallas kernels, layer_call(): pl.pallas_call(partial(layer_kernel, geo), out_shape=(shape(tok.shape, bf...  235 us
    unnamed x10, local copies, waits for them, and re-layouts  7.01 us

profile of v6, /device:TPU:0, one launch (start us, length us, event | category | flops | bytes accessed | tf_op | source)
XLA Modules:
  0.0 244.9 jit_solution(10680039264967395614)
XLA Ops:
  0.6 234.7 %encoder_layer.1 = (bf16[4,512,768]{2,1,0:T(8,128)(2,1)}, bf16[4,512,768]{2,1,0:T(8,128)(2,1)}, f32[4,512,768]{2,1,0:T(8,128)}, f32[96,768]{1,0:T(8,128)}, f32[96,768]{1,0:T(8,128)}, /*index=5*/f32[8,128]{1,0:T(8,128)}) custom-call(bf16[4,512,768]{2,1,0:T(8,128)(2,1)} %tok.1, bf16[4,512,768]{2,1,0:T(8,128)(2,1)} %cot.1, bf16[96,768]{1,0:T(8,128)(2,1)} %bitcast.21, ...), custom_call_target="tpu_custom_call" | custom-call | tf_op jit(solution)/shard_map/encoder_layer/pallas_call | solution.py:943
  235.4 1.2 slice_bitcast_fusion.5
  236.5 1.4 slice_bitcast_fusion
  237.9 0.0 copy-start
  237.9 3.9 %copy.28 = bf16[4,512,768]{2,1,0:T(8,128)(2,1)} copy(bf16[4,512,768]{2,1,0:T(8,128)(2,1)} %get-tuple-element.35) | data formatting | bytes 6291456
  241.8 0.0 copy-done
  241.8 0.0 copy-start.2
  241.8 0.0 copy-start.1
  241.8 1.7 copy.29
  243.5 0.0 copy-done.2
  243.5 0.7 copy.30
  244.2 0.0 copy-done.1
  244.2 0.7 copy.31
Async XLA Ops:
  237.9 3.9 %copy-start = (bf16[4,512,768]{2,1,0:T(8,128)(2,1)S(1)}, bf16[4,512,768]{2,1,0:T(8,128)(2,1)}, u32[]{:S(2)}) copy-start(bf16[4,512,768]{2,1,0:T(8,128)(2,1)} %get-tuple-element.36) | copy-start | bytes 9437188
  241.8 1.7 copy-start.2
  241.8 2.4 copy-start.1

commit v7 on v6

--- a/solution.py
+++ b/solution.py
@@ -624,7 +624,9 @@
         mixed_job(i)
         tell(free2, i)
         ffn_hidden(lambda at: tokv[i, at, :], nbuf, sbuf, alow, hid, slope, weight, vec, bias_in, rows_step)
-        lax.fori_loop(i + 1 + i // 3, i + 2 + i // 2 + i // 3, sequence_job, 0)
+        @pl.when(i != 1)
+        def _():
+            sequence_job(i + 1 + (i + 1) // 2, 0)
 
         @pl.when(i == 0)
         def _():
@@ -648,6 +650,11 @@
         ffn_backward(nbuf, sbuf, hid, slope, acc, glow, weight, bsum, vec, sums, rows_step, put)
         row_copy(i).start()
         hidden_job(i + jobs)
+
+        @pl.when(i < 3)
+        def _():
+            sequence_job(i + 2 + i // 2, 0)
+
         ffn_grads(alow, hid, slope, glow, dw)
         row_copy(i).wait()
         return carry
@@ -817,19 +824,26 @@
     vec_step(1)
     pl.semaphore_wait(ready.at[1], 1)
     pl.semaphore_wait(ready.at[2], 1)
-    lax.fori_loop(0, planes, first_step, 0)
+    first_step(0, 0)
     final(0, 0)
     tell(free2, jobs)
+    lax.fori_loop(1, last, first_step, 0)
+    next_step(0, 0)
     vec_step(2)
-    lax.fori_loop(0, planes // 2, next_step, 0)
+    final(2, 0)
+    next_step(1, 0)
+    final(1, 0)
+    lax.fori_loop(2, last, next_step, 0)
+    z_step(0, 0)
+    first_step(last, 0)
+    vec_step(3)
+    z_step(1, 0)
     sequence_job(2 * jobs - 1, 0)
-    final(1, 0)
-    lax.fori_loop(planes // 2, planes, next_step, 0)
-    vec_step(3)
-    final(2, 0)
-    lax.fori_loop(0, planes, z_step, 0)
+    lax.fori_loop(2, last, z_step, 0)
+    next_step(last, 0)
     late_step()
     final(3, 0)
+    z_step(last, 0)
     own_most, own_rest = owned_most(quad, last), owned_rest(quad, last)
     for v in range(last):
         z_copy(v).wait_recv()

time: 245 us -> 238 us (0.971)
  Pallas kernels: 235 us -> 227 us
    pallas_call x1, Pallas kernels: 235 us -> 227 us  [layer_call(): pl.pallas_call(partial(layer_kernel, geo), out_shape=(shape(tok.shape, bf...]
where the time goes in v7:
time: 238 us
  Pallas kernels  227 us (95%)
  local copies, waits for them, and re-layouts  9.58 us (4%)
    pallas_call x1, Pallas kernels, layer_call(): pl.pallas_call(partial(layer_kernel, geo), out_shape=(shape(tok.shape, bf...  227 us
    unnamed x10, local copies, waits for them, and re-layouts  7.01 us

profile of v7, /device:TPU:0, one launch (start us, length us, event | category | flops | bytes accessed | tf_op | source)
XLA Modules:
  0.0 237.7 jit_solution(4682036466852529405)
XLA Ops:
  0.6 227.5 %encoder_layer.1 = (bf16[4,512,768]{2,1,0:T(8,128)(2,1)}, bf16[4,512,768]{2,1,0:T(8,128)(2,1)}, f32[4,512,768]{2,1,0:T(8,128)}, f32[96,768]{1,0:T(8,128)}, f32[96,768]{1,0:T(8,128)}, /*index=5*/f32[8,128]{1,0:T(8,128)}) custom-call(bf16[4,512,768]{2,1,0:T(8,128)(2,1)} %tok.1, bf16[4,512,768]{2,1,0:T(8,128)(2,1)} %cot.1, bf16[96,768]{1,0:T(8,128)(2,1)} %bitcast.21, ...), custom_call_target="tpu_custom_call" | custom-call | tf_op jit(solution)/shard_map/encoder_layer/pallas_call | solution.py:957
  228.1 1.2 slice_bitcast_fusion.5
  229.3 1.4 slice_bitcast_fusion
  230.7 0.0 copy-start
  230.7 3.9 %copy.28 = bf16[4,512,768]{2,1,0:T(8,128)(2,1)} copy(bf16[4,512,768]{2,1,0:T(8,128)(2,1)} %get-tuple-element.35) | data formatting | bytes 6291456
  234.6 0.0 copy-done
  234.6 0.0 copy-start.2
  234.6 0.0 copy-start.1
  234.6 1.7 copy.29
  236.3 0.0 copy-done.2
  236.3 0.7 copy.30
  237.0 0.0 copy-done.1
  237.0 0.7 copy.31
Async XLA Ops:
  230.7 3.9 %copy-start = (bf16[4,512,768]{2,1,0:T(8,128)(2,1)S(1)}, bf16[4,512,768]{2,1,0:T(8,128)(2,1)}, u32[]{:S(2)}) copy-start(bf16[4,512,768]{2,1,0:T(8,128)(2,1)} %get-tuple-element.36) | copy-start | bytes 9437188
  234.6 1.7 copy-start.2
  234.6 2.4 %copy-start.1 = (f32[96,768]{1,0:T(8,128)S(1)}, f32[96,768]{1,0:T(8,128)}, u32[]{:S(2)}) copy-start(f32[96,768]{1,0:T(8,128)} %get-tuple-element.39) | copy-start | bytes 884740

commit v8 on v7

--- a/solution.py
+++ b/solution.py
@@ -274,9 +274,18 @@
         a, b = ((hp_all, hp), (wd_all, wd), (cp_all, cp))[k - jobs]
         return pltpu.make_async_copy(a, b, load.at[k])
 
-    for k in (jobs, 0, 1, jobs + 1, 2, 3, jobs + 2):
-        load_of(k).start()
-
+    barrier = pltpu.get_barrier_semaphore()
+
+    def greet(d, carry):
+        pl.semaphore_signal(barrier, inc=1, device_id=(peer(d), plane), device_id_type=MESH)
+        return carry
+
+    def greet_z(d, carry):
+        pl.semaphore_signal(barrier, inc=1, device_id=(me, lax.rem(plane + d, planes)), device_id_type=MESH)
+        return carry
+
+    lax.fori_loop(1, parts, greet, 0)
+    lax.fori_loop(1, planes, greet_z, 0)
     core, quad = lax.rem(me, 2), me // 2
     quads = parts // 2
     x, y = lax.rem(quad, 2), quad // 2
@@ -296,6 +305,8 @@
     )
     for copy in own_loads:
         copy.start()
+    for k in (jobs, 0, 1, jobs + 1, 2, 3, jobs + 2):
+        load_of(k).start()
 
     owner = me * planes + plane
     part = width // (parts * planes)
@@ -313,18 +324,6 @@
     placed = jnp.where(is_bias, jnp.broadcast_to(bias8[0:1], (16, width)), placed)
     va[0] = placed.astype(bf16)
 
-    barrier = pltpu.get_barrier_semaphore()
-
-    def greet(d, carry):
-        pl.semaphore_signal(barrier, inc=1, device_id=(peer(d), plane), device_id_type=MESH)
-        return carry
-
-    def greet_z(d, carry):
-        pl.semaphore_signal(barrier, inc=1, device_id=(me, lax.rem(plane + d, planes)), device_id_type=MESH)
-        return carry
-
-    lax.fori_loop(1, parts, greet, 0)
-    lax.fori_loop(1, planes, greet_z, 0)
     pl.semaphore_wait(barrier, parts - 1 + planes - 1)
 
     def remote(send, recv, ss, rs, k, d):
@@ -678,9 +677,10 @@
     def core_copy(v):
         return send(w1.at[v], w0.at[v], s_core.at[v], r_core.at[v], partner)
 
+    staged = 2 * quads * rest_rows
+
     def first_copy(v, m):
-        at = pl.ds(2 * m, 2)
-        return send(w1.at[2 + v // 2, lax.rem(v, 2), at, head], w1.at[v // 2, lax.rem(v, 2), at, head],
+        return send(hid.at[v, pl.ds(staged + 2 * m * most, 2 * most)], slope.at[v, pl.ds(2 * m * most, 2 * most)],
                     s_first.at[v, m], r_first.at[v, m], (x_peer, y_peer)[m])
 
     def next_copy(v, m):
@@ -735,7 +735,8 @@
         for k in range(2):
             for m in range(2):
                 q = 2 * k + 1 - x if m == 0 else 2 * (1 - y) + k
-                w1[2 + v // 2, lax.rem(v, 2), 2 * m + k, 0:most, :] = dw[m, owned_most(q, v)].astype(bf16)
+                at = pl.ds(staged + (2 * m + k) * most, most)
+                hid[v, at, :] = dw[m, owned_most(q, v)].astype(bf16)
         for m in range(2):
             first_copy(v, m).start()
         return carry
@@ -746,7 +747,7 @@
         for k in range(2):
             for m in range(2):
                 q = 2 * k + x if m == 0 else 2 * y + k
-                dw[m, owned_most(q, v)] += w1[v // 2, lax.rem(v, 2), 2 * m + k, 0:most, :].astype(f32)
+                dw[m, owned_most(q, v)] += slope[v, (2 * m + k) * most:(2 * m + k + 1) * most, :].astype(f32)
         for m in range(2):
             q = 2 * (1 - y) + x if m == 0 else 2 * y + 1 - x
             w0[0, v // 2, 2 * lax.rem(v, 2) + m, 0:most, :] = dw[m, owned_most(q, v)].astype(bf16)
@@ -809,18 +810,11 @@
         return carry
 
     gather_sent()
-    pl.semaphore_signal(ready.at[0], inc=1, device_id=partner, device_id_type=MESH)
+    for n, to in enumerate((partner, x_peer, y_peer)):
+        pl.semaphore_signal(ready.at[n], inc=1, device_id=to, device_id_type=MESH)
     pl.semaphore_wait(ready.at[0], 1)
     lax.fori_loop(0, planes, core_step, 0)
     vec_step(0)
-
-    def core_sent(v, carry):
-        core_copy(v).wait_send()
-        return carry
-
-    lax.fori_loop(0, planes, core_sent, 0)
-    pl.semaphore_signal(ready.at[1], inc=1, device_id=x_peer, device_id_type=MESH)
-    pl.semaphore_signal(ready.at[2], inc=1, device_id=y_peer, device_id_type=MESH)
     vec_step(1)
     pl.semaphore_wait(ready.at[1], 1)
     pl.semaphore_wait(ready.at[2], 1)
@@ -869,6 +863,7 @@
     small[...] = jnp.where(row8 == 5, mine[:, 0:128], rows8[:, 0:128])
 
     def sent(v, carry):
+        core_copy(v).wait_send()
         for m in range(2):
             first_copy(v, m).wait_send()
             next_copy(v, m).wait_send()

time: 238 us -> 238 us (level)
  no operation moved by 1% of the time
where the time goes in v8:
time: 238 us; the launch traced here: 237 us
  Pallas kernels  227 us (95%)
  local copies, waits for them, and re-layouts  9.58 us (4%)
    pallas_call x1, Pallas kernels, layer_call(): pl.pallas_call(partial(layer_kernel, geo), out_shape=(shape(tok.shape, bf...  227 us
    unnamed x10, local copies, waits for them, and re-layouts  7.01 us

profile of v8, /device:TPU:0, one launch (start us, length us, event | category | flops | bytes accessed | tf_op | source)
XLA Modules:
  0.0 237.5 jit_solution(6024599106773491325)
XLA Ops:
  0.6 227.2 %encoder_layer.1 = (bf16[4,512,768]{2,1,0:T(8,128)(2,1)}, bf16[4,512,768]{2,1,0:T(8,128)(2,1)}, f32[4,512,768]{2,1,0:T(8,128)}, f32[96,768]{1,0:T(8,128)}, f32[96,768]{1,0:T(8,128)}, /*index=5*/f32[8,128]{1,0:T(8,128)}) custom-call(bf16[4,512,768]{2,1,0:T(8,128)(2,1)} %tok.1, bf16[4,512,768]{2,1,0:T(8,128)(2,1)} %cot.1, bf16[96,768]{1,0:T(8,128)(2,1)} %bitcast.21, ...), custom_call_target="tpu_custom_call" | custom-call | tf_op jit(solution)/shard_map/encoder_layer/pallas_call | solution.py:952
  227.9 1.2 slice_bitcast_fusion.5
  229.1 1.4 slice_bitcast_fusion
  230.5 0.0 copy-start
  230.5 3.9 %copy.28 = bf16[4,512,768]{2,1,0:T(8,128)(2,1)} copy(bf16[4,512,768]{2,1,0:T(8,128)(2,1)} %get-tuple-element.35) | data formatting | bytes 6291456
  234.4 0.0 copy-done
  234.4 0.0 copy-start.2
  234.4 0.0 copy-start.1
  234.4 1.7 copy.29
  236.0 0.0 copy-done.2
  236.0 0.7 copy.30
  236.8 0.0 copy-done.1
  236.8 0.7 copy.31
Async XLA Ops:
  230.5 3.9 %copy-start = (bf16[4,512,768]{2,1,0:T(8,128)(2,1)S(1)}, bf16[4,512,768]{2,1,0:T(8,128)(2,1)}, u32[]{:S(2)}) copy-start(bf16[4,512,768]{2,1,0:T(8,128)(2,1)} %get-tuple-element.36) | copy-start | bytes 9437188
  234.4 1.7 copy-start.2
  234.4 2.4 %copy-start.1 = (f32[96,768]{1,0:T(8,128)S(1)}, f32[96,768]{1,0:T(8,128)}, u32[]{:S(2)}) copy-start(f32[96,768]{1,0:T(8,128)} %get-tuple-element.39) | copy-start | bytes 884740
